TPU v7x, 32 devices: a whole 2x2x4 slice. The times are simulated.
32 devices in a mesh: dp: 2 (over x), head: 16 (over z, y, core).
Axes of the slice: x: 2, y: 2, z: 4, core: 2. Of those that a mesh axis runs over, the one named last changes fastest.
Arguments:
- tokens: bfloat16 [8192, 1024], P(('dp', 'head')), may hold values from -6 to 6
- lengths: int32 [2, 4], P('dp'), may hold values from 1 to 4, 8 in all within a row
- w_query: bfloat16 [1024, 1024], P(None, 'head'), may hold values from -0.1875 to 0.1875
- w_key: bfloat16 [1024, 1024], P(None, 'head'), may hold values from -0.1875 to 0.1875
- w_value: bfloat16 [1024, 1024], P(None, 'head'), may hold values from -0.1875 to 0.1875
- s_qk: float32 [1024], P('head'), may hold values from 0.8 to 1.6
- w_out: bfloat16 [1024, 1024], P('head'), may hold values from -0.1875 to 0.1875
- up_weight: bfloat16 [4096, 1024], P(('dp', 'head')), may hold values from -0.1875 to 0.1875
- gate_weight: bfloat16 [4096, 1024], P(('dp', 'head')), may hold values from -0.1875 to 0.1875
- down_weight: bfloat16 [4096, 1024], P(('dp', 'head')), may hold values from -0.09375 to 0.09375
- s_up: bfloat16 [4096], P(('dp', 'head')), may hold values from 0.5 to 1.5
- s_gate: bfloat16 [4096], P(('dp', 'head')), may hold values from 0.5 to 1.5
- alpha_attn: float32 [1024], replicated, may hold values from 0.1 to 0.9
- alpha_mlp: float32 [1024], replicated, may hold values from 0.1 to 0.9
- cotangent: bfloat16 [8192, 1024], P(('dp', 'head')), may hold values from -6 to 6
Outputs:
- mixed: bfloat16 [8192, 1024], P(('dp', 'head'))
- tokens_grad: bfloat16 [8192, 1024], P(('dp', 'head'))
- w_query_grad: float32 [1024, 1024], P(None, 'head')
- w_key_grad: float32 [1024, 1024], P(None, 'head')
- w_value_grad: float32 [1024, 1024], P(None, 'head')
- s_qk_grad: float32 [1024], P('head')
- w_out_grad: float32 [1024, 1024], P('head')
- up_grad: float32 [4096, 1024], P(('dp', 'head'))
- gate_grad: float32 [4096, 1024], P(('dp', 'head'))
- down_grad: float32 [4096, 1024], P(('dp', 'head'))
- s_up_grad: float32 [4096], P(('dp', 'head'))
- s_gate_grad: float32 [4096], P(('dp', 'head'))
- alpha_attn_grad: float32 [1024], replicated
- alpha_mlp_grad: float32 [1024], replicated
Inputs may be any that keep to these rules, and one draw needn't show every extreme that they name: Row g gives, in blocks of 512 tokens, the lengths of the 4 sequences that fill the g-th group of 4096 tokens in order; each row sums to 8 and its largest entry is 4.
All inputs are finite; a program needn't handle non-finite values.
Results may differ from a plain program's by a relative error of at most 0.02.
Values may be sent and summed in bfloat16 or wider, within the bound.
A program may use at most 192 MiB of HBM per device.

v0:
```python
import math

import jax
import jax.numpy as jnp
from jax import lax
from jax.sharding import PartitionSpec as P

HEAD_DIM = 64
BLOCK = 512
MAXSEQ = 4096


epsilon = 1e-06


def sphere(values):
    return values * lax.rsqrt(jnp.mean(values * values, axis=-1, keepdims=True) + epsilon)


def layout(lengths_row, group_rows):
    ends = jnp.cumsum(lengths_row) * BLOCK
    starts = ends - lengths_row * BLOCK
    row_index = jnp.arange(group_rows, dtype=jnp.int32)
    seq_index = jnp.sum((row_index[:, None] >= ends[None, :]).astype(jnp.int32), axis=1)
    member = seq_index[:, None] == jnp.arange(lengths_row.shape[0], dtype=jnp.int32)[None, :]
    first_row = jnp.sum(jnp.where(member, starts[None, :], 0), axis=1)
    return (seq_index, row_index - first_row)


def rotation_angles(places):
    half_dim = HEAD_DIM // 2
    frequency = jnp.exp(
        jnp.arange(half_dim, dtype=jnp.float32) * (-2.0 * math.log(10000.0) / HEAD_DIM)
    )
    return places.astype(jnp.float32)[:, None] * frequency[None, :]


def rotate(heads, angles):
    half_dim = heads.shape[-1] // 2
    cosine = jnp.cos(angles)[:, None, :]
    sine_part = jnp.sin(angles)[:, None, :]
    first_half = heads[..., :half_dim]
    second_half = heads[..., half_dim:]
    return jnp.concatenate(
        [
            first_half * cosine - second_half * sine_part,
            second_half * cosine + first_half * sine_part,
        ],
        axis=-1,
    )


def head_features(projected, head_gain, angles):
    count_rows = projected.shape[0]
    heads = projected.reshape(count_rows, -1, HEAD_DIM)
    heads = sphere(rotate(heads, angles)) * head_gain.reshape(-1, HEAD_DIM)[None, :, :]
    return heads.reshape(count_rows, -1)


def product(left, right):
    return jnp.dot(left, right, preferred_element_type=jnp.float32)


def product_left(left, right):
    return lax.dot_general(
        left, right, (((0,), (0,)), ((), ())), preferred_element_type=jnp.float32
    )


def product_right(left, right):
    return lax.dot_general(
        left, right, (((1,), (1,)), ((), ())), preferred_element_type=jnp.float32
    )


def mlp_core(up_proj, gate_proj, up_scale, gate_scale):
    gated = gate_proj * gate_scale
    return up_proj * up_scale * (gated * jax.nn.sigmoid(gated))


def front(branch, own_tokens, alpha_attn):
    return sphere(own_tokens + alpha_attn * (sphere(branch) - own_tokens))


def finish(hidden, mlp_out, alpha_mlp):
    return sphere(hidden + alpha_mlp * (sphere(mlp_out) - hidden))


def block_geometry(seq_index, block_index, reach):
    key_start = jnp.maximum((block_index + 1) * BLOCK - reach, 0)
    query_seq = lax.dynamic_slice_in_dim(seq_index, block_index * BLOCK, BLOCK, 0)
    key_seq = lax.dynamic_slice_in_dim(seq_index, key_start, reach, 0)
    query_row = block_index * BLOCK + jnp.arange(BLOCK, dtype=jnp.int32)
    key_row = key_start + jnp.arange(reach, dtype=jnp.int32)
    allowed = (query_seq[:, None] == key_seq[None, :]) & (key_row[None, :] <= query_row[:, None])
    return (key_start, allowed)


def block_scores(query_heads, key_heads, block_index, key_start, reach, allowed):
    query_rows = lax.dynamic_slice_in_dim(query_heads, block_index * BLOCK, BLOCK, 0)
    key_rows = lax.dynamic_slice_in_dim(key_heads, key_start, reach, 0)
    scores = jnp.einsum(
        "qhd,khd->hqk", query_rows, key_rows, preferred_element_type=jnp.float32
    ) / math.sqrt(HEAD_DIM)
    return (jnp.where(allowed[None, :, :], scores, -1e30), query_rows, key_rows)


def shards(
    tokens,
    lengths,
    w_query,
    w_key,
    w_value,
    s_qk,
    w_out,
    up_weight,
    gate_weight,
    down_weight,
    s_up,
    s_gate,
    alpha_attn,
    alpha_mlp,
    cotangent,
):
    group_tokens = lax.all_gather(tokens, "head", axis=0, tiled=True)
    group_rows = group_tokens.shape[0]
    reach = min(MAXSEQ, group_rows // 2)
    blocks = group_rows // BLOCK
    width = w_query.shape[1]
    local_heads = width // HEAD_DIM
    seq_index, places = layout(lengths[0], group_rows)
    angles = rotation_angles(places)
    joint_weight = jnp.concatenate([w_query, w_key, w_value], axis=1)
    projected = product(group_tokens, joint_weight)
    query_proj = projected[:, :width]
    key_proj = projected[:, width : 2 * width]
    value_heads = (
        projected[:, 2 * width :].astype(jnp.bfloat16).reshape(group_rows, local_heads, HEAD_DIM)
    )
    query_unit, query_pull = jax.vjp(
        lambda proj_part, head_gain: head_features(proj_part, head_gain, angles), query_proj, s_qk
    )
    key_unit, key_pull = jax.vjp(
        lambda proj_part, head_gain: head_features(proj_part, head_gain, angles), key_proj, s_qk
    )
    query_heads = query_unit.astype(jnp.bfloat16).reshape(group_rows, local_heads, HEAD_DIM)
    key_heads = key_unit.astype(jnp.bfloat16).reshape(group_rows, local_heads, HEAD_DIM)

    def forward_block(block_index):
        key_start, allowed = block_geometry(seq_index, block_index, reach)
        scores, query_rows, key_rows = block_scores(
            query_heads, key_heads, block_index, key_start, reach, allowed
        )
        value_rows = lax.dynamic_slice_in_dim(value_heads, key_start, reach, 0)
        highest = jnp.max(scores, axis=-1, keepdims=True)
        shifted = jnp.exp(scores - highest)
        totals = jnp.sum(shifted, axis=-1, keepdims=True)
        weights = (shifted / totals).astype(jnp.bfloat16)
        attended = jnp.einsum(
            "hqk,khd->qhd", weights, value_rows, preferred_element_type=jnp.float32
        )
        return (attended.astype(jnp.bfloat16), (highest + jnp.log(totals))[:, :, 0])

    head_blocks, log_totals = lax.map(forward_block, jnp.arange(blocks, dtype=jnp.int32))
    head_out = head_blocks.reshape(group_rows, width)
    branch = lax.psum_scatter(product(head_out, w_out), "head", scatter_dimension=0, tiled=True)
    own_tokens = tokens.astype(jnp.float32)
    hidden, front_pull = jax.vjp(front, branch, own_tokens, alpha_attn)
    hidden_low = hidden.astype(jnp.bfloat16)
    up_full, gate_full, down_full, up_scale, gate_scale = (
        lax.all_gather(up_weight, ("dp", "head"), axis=0, tiled=True),
        lax.all_gather(gate_weight, ("dp", "head"), axis=0, tiled=True),
        lax.all_gather(down_weight, ("dp", "head"), axis=0, tiled=True),
        lax.all_gather(s_up, ("dp", "head"), axis=0, tiled=True),
        lax.all_gather(s_gate, ("dp", "head"), axis=0, tiled=True),
    )
    up_proj = product_right(hidden_low, up_full)
    gate_proj = product_right(hidden_low, gate_full)
    inner, core_pull = jax.vjp(
        mlp_core, up_proj, gate_proj, up_scale.astype(jnp.float32), gate_scale.astype(jnp.float32)
    )
    inner_low = inner.astype(jnp.bfloat16)
    mlp_out = product(inner_low, down_full)
    mixed, finish_pull = jax.vjp(finish, hidden, mlp_out, alpha_mlp)
    up_full, gate_full, down_full = (
        lax.all_gather(up_weight, ("dp", "head"), axis=0, tiled=True),
        lax.all_gather(gate_weight, ("dp", "head"), axis=0, tiled=True),
        lax.all_gather(down_weight, ("dp", "head"), axis=0, tiled=True),
    )
    hidden_grad, mlp_out_grad, alpha_mlp_grad = finish_pull(cotangent.astype(jnp.float32))
    mlp_out_low = mlp_out_grad.astype(jnp.bfloat16)
    down_grad = product_left(inner_low, mlp_out_low)
    inner_grad = product_right(mlp_out_low, down_full)
    up_proj_grad, gate_proj_grad, up_scale_grad, gate_scale_grad = core_pull(inner_grad)
    up_low = up_proj_grad.astype(jnp.bfloat16)
    gate_low = gate_proj_grad.astype(jnp.bfloat16)
    hidden_grad = hidden_grad + product(up_low, up_full) + product(gate_low, gate_full)
    up_grad = product_left(up_low, hidden_low)
    gate_grad = product_left(gate_low, hidden_low)
    branch_grad, token_grad, alpha_attn_grad = front_pull(hidden_grad)
    branch_low = branch_grad.astype(jnp.bfloat16)
    group_branch = lax.all_gather(branch_low, "head", axis=0, tiled=True)
    head_grad = product_right(group_branch, w_out).astype(jnp.bfloat16)
    out_grad = product_left(head_out, group_branch)
    head_grad = head_grad.reshape(group_rows, local_heads, HEAD_DIM)

    def backward_block(carry, block_index):
        key_acc, value_acc = carry
        key_start, allowed = block_geometry(seq_index, block_index, reach)
        scores, query_rows, key_rows = block_scores(
            query_heads, key_heads, block_index, key_start, reach, allowed
        )
        value_rows = lax.dynamic_slice_in_dim(value_heads, key_start, reach, 0)
        grad_rows = lax.dynamic_slice_in_dim(head_grad, block_index * BLOCK, BLOCK, 0)
        log_row = lax.dynamic_index_in_dim(log_totals, block_index, 0, keepdims=False)
        probs = jnp.exp(scores - log_row[:, :, None])
        prob_grad = jnp.einsum(
            "qhd,khd->hqk", grad_rows, value_rows, preferred_element_type=jnp.float32
        )
        inner_sum = jnp.sum(probs * prob_grad, axis=-1, keepdims=True)
        score_grad = (probs * (prob_grad - inner_sum)).astype(jnp.bfloat16)
        root = math.sqrt(HEAD_DIM)
        query_grad = (
            jnp.einsum("hqk,khd->qhd", score_grad, key_rows, preferred_element_type=jnp.float32)
            / root
        )
        key_grad = (
            jnp.einsum("hqk,qhd->khd", score_grad, query_rows, preferred_element_type=jnp.float32)
            / root
        )
        value_part = jnp.einsum(
            "hqk,qhd->khd",
            probs.astype(jnp.bfloat16),
            grad_rows,
            preferred_element_type=jnp.float32,
        )
        key_acc = lax.dynamic_update_slice_in_dim(
            key_acc, lax.dynamic_slice_in_dim(key_acc, key_start, reach, 0) + key_grad, key_start, 0
        )
        value_acc = lax.dynamic_update_slice_in_dim(
            value_acc,
            lax.dynamic_slice_in_dim(value_acc, key_start, reach, 0) + value_part,
            key_start,
            0,
        )
        return ((key_acc, value_acc), query_grad)

    zeros_heads = jnp.zeros((group_rows, local_heads, HEAD_DIM), jnp.float32)
    (key_unit_grad, value_grad), query_blocks = lax.scan(
        backward_block, (zeros_heads, zeros_heads), jnp.arange(blocks, dtype=jnp.int32)
    )
    query_proj_grad, query_gain_grad = query_pull(query_blocks.reshape(group_rows, width))
    key_proj_grad, key_gain_grad = key_pull(key_unit_grad.reshape(group_rows, width))
    joint_grad = jnp.concatenate(
        [query_proj_grad, key_proj_grad, value_grad.reshape(group_rows, width)], axis=1
    ).astype(jnp.bfloat16)
    joint_weight_grad = product_left(group_tokens, joint_grad)
    token_attn_grad = lax.psum_scatter(
        product_right(joint_grad, joint_weight).astype(jnp.bfloat16),
        "head",
        scatter_dimension=0,
        tiled=True,
    ).astype(jnp.float32)
    attn_sums = (
        lax.psum(joint_weight_grad[:, :width].astype(jnp.bfloat16), "dp").astype(jnp.float32),
        lax.psum(joint_weight_grad[:, width : 2 * width].astype(jnp.bfloat16), "dp").astype(
            jnp.float32
        ),
        lax.psum(joint_weight_grad[:, 2 * width :].astype(jnp.bfloat16), "dp").astype(jnp.float32),
        lax.psum((query_gain_grad + key_gain_grad).astype(jnp.bfloat16), "dp").astype(jnp.float32),
        lax.psum(out_grad.astype(jnp.bfloat16), "dp").astype(jnp.float32),
    )
    mlp_sums = (
        lax.psum_scatter(up_grad, ("dp", "head"), scatter_dimension=0, tiled=True),
        lax.psum_scatter(gate_grad, ("dp", "head"), scatter_dimension=0, tiled=True),
        lax.psum_scatter(down_grad, ("dp", "head"), scatter_dimension=0, tiled=True),
        lax.psum_scatter(up_scale_grad, ("dp", "head"), scatter_dimension=0, tiled=True),
        lax.psum_scatter(gate_scale_grad, ("dp", "head"), scatter_dimension=0, tiled=True),
    )
    alpha_sums = lax.psum((alpha_attn_grad, alpha_mlp_grad), ("dp", "head"))
    return (
        mixed.astype(jnp.bfloat16),
        (token_grad + token_attn_grad).astype(jnp.bfloat16),
        attn_sums[0],
        attn_sums[1],
        attn_sums[2],
        attn_sums[3],
        attn_sums[4],
        mlp_sums[0],
        mlp_sums[1],
        mlp_sums[2],
        mlp_sums[3],
        mlp_sums[4],
        alpha_sums[0],
        alpha_sums[1],
    )


def solution(mesh):
    in_specs = (
        P(("dp", "head"), None),
        P("dp", None),
        P(None, "head"),
        P(None, "head"),
        P(None, "head"),
        P("head"),
        P("head", None),
        P(("dp", "head"), None),
        P(("dp", "head"), None),
        P(("dp", "head"), None),
        P(("dp", "head")),
        P(("dp", "head")),
        P(),
        P(),
        P(("dp", "head"), None),
    )
    out_specs = (
        P(("dp", "head"), None),
        P(("dp", "head"), None),
        P(None, "head"),
        P(None, "head"),
        P(None, "head"),
        P("head"),
        P("head", None),
        P(("dp", "head"), None),
        P(("dp", "head"), None),
        P(("dp", "head"), None),
        P(("dp", "head")),
        P(("dp", "head")),
        P(),
        P(),
    )
    return jax.shard_map(shards, mesh=mesh, in_specs=in_specs, out_specs=out_specs, check_vma=False)
```

profile of v0, /device:TPU:0, one launch (start us, length us, event | category | flops | bytes accessed | tf_op | source)
XLA Modules:
  0.0 1512.9 jit_solution(17210577638115528813)
XLA Ops:
  13.4 75.3 %all-gather.8.cloned.1.call-done = bf16[4096,1024]{1,0:T(8,128)(2,1)} async-done(((bf16[256,1024]{1,0:T(8,128)(2,1)}), bf16[4096,1024]{1,0:T(8,128)(2,1)}) %all-gather.8.cloned.1.call-update) | async-done | bytes 8388624 | tf_op jit(solution)/shard_map/all_gather | solution.py:125
  88.7 6.3 convolution_bitcast_fusion.1
  100.8 57.2 %while.30 = (s32[]{:T(128)}, bf16[8,512,1,64]{1,3,2,0:T(8,128)(2,1)S(1)}, f32[8,1,512]{2,1,0:T(1,128)S(1)}, s32[8]{0:T(128)S(1)}, bf16[4096,1,64]{0,2,1:T(8,128)...) while((s32[]{:T(128)}, ...), condition=%wide.region_8.9_spmd, body=%wide.region_5.8_spmd.sunk | while | flops 280004608 | bytes 13311759 | solution.py:164
  159.0 8.1 fusion.87
  168.9 38.6 %all-gather.1 = bf16[32,1,128]{2,1,0:T(2,128)(2,1)S(1)} all-gather(bf16[1,1,128]{2,1,0:T(2,128)(2,1)S(1)} %bitcast.206), channel_id=1, replica_groups=mesh['dp'=2,'head'=16] {'dp','head'}, dimensions={0}, use_global_device_ids=true | all-gather | bytes 8448 | tf_op jit(solution)/shard_map/all_gather | solution.py:175
  207.5 38.2 %all-gather = bf16[32,1,128]{2,1,0:T(2,128)(2,1)S(1)} all-gather(bf16[1,1,128]{2,1,0:T(2,128)(2,1)S(1)} %bitcast.207), channel_id=1, replica_groups=mesh['dp'=2,'head'=16] {'dp','head'}, dimensions={0}, use_global_device_ids=true | all-gather | bytes 8448 | tf_op jit(solution)/shard_map/all_gather | solution.py:174
  245.8 134.3 %reduce-scatter.6.cloned.1.call-done = f32[256,1024]{1,0:T(8,128)} async-done(((f32[4096,1024]{1,0:T(8,128)}), f32[256,1024]{1,0:T(8,128)}) %reduce-scatter.6.cloned.1.call-update) | async-done | bytes 1048592 | tf_op jit(solution)/shard_map/reduce_scatter | solution.py:166
  383.4 7.9 fusion.88
  391.4 25.3 %all-gather.10.cloned.1.call-done = bf16[4096,1024]{1,0:T(8,128)(2,1)} async-done(((bf16[128,1024]{1,0:T(8,128)(2,1)}), bf16[4096,1024]{1,0:T(8,128)(2,1)}) %all-gather.10.cloned.1.call-update) | async-done | bytes 8388624 | tf_op jit(solution)/shard_map/all_gather | solution.py:171
  416.7 10.2 multiply_convert_fusion.3
  426.9 68.4 %all-gather.14.cloned.1.call-done = bf16[4096,1024]{1,0:T(8,128)(2,1)} async-done(((bf16[128,1024]{1,0:T(8,128)(2,1)}), bf16[4096,1024]{1,0:T(8,128)(2,1)}) %all-gather.14.cloned.1.call-update) | async-done | bytes 8388624 | tf_op jit(solution)/shard_map/all_gather | solution.py:173
  495.3 6.5 multiply_reduce_fusion.13
  504.8 8.6 multiply_reduce_fusion.1
  513.4 8.1 convolution_add_fusion.1
  528.7 71.9 %all-gather.16.cloned.1.call-done = bf16[4096,1024]{1,0:T(8,128)(2,1)} async-done(((bf16[256,1024]{1,0:T(8,128)(2,1)}), bf16[4096,1024]{1,0:T(8,128)(2,1)}) %all-gather.16.cloned.1.call-update) | async-done | bytes 8388624 | tf_op jit(solution)/shard_map/all_gather | solution.py:202
  600.6 6.8 fusion.39
  609.6 208.9 %while.31 = (s32[]{:T(128)}, f32[4096,1,64]{0,2,1:T(8,128)}, f32[4096,1,64]{0,2,1:T(8,128)}, f32[8,512,1,64]{1,3,2,0:T(8,128)}, s32[8]{0:T(128)S(1)}, /*index=5*...) while((s32[]{:T(128)}, f32[4096,1,64]{0,2,1:T(8,128)}, ...), condition=%wide.region_20.21_spmd, body=%wide.region_18.20_spmd.sunk | while | flops 684099584 | bytes 83031024 | solution.py:249
  611.7 3.7 fusion.147
  617.5 4.3 multiply_reduce_fusion.19
  625.2 3.4 dynamic_update_slice.44
  637.6 3.7 fusion.147
  643.5 4.3 multiply_reduce_fusion.19
  651.1 3.4 dynamic_update_slice.44
  663.6 3.7 fusion.147
  669.4 4.3 multiply_reduce_fusion.19
  677.1 3.4 dynamic_update_slice.44
  689.6 3.7 fusion.147
  695.4 4.3 multiply_reduce_fusion.19
  703.0 3.4 dynamic_update_slice.44
  715.5 3.7 fusion.147
  721.4 4.3 multiply_reduce_fusion.19
  729.0 3.4 dynamic_update_slice.44
  742.6 3.7 fusion.147
  748.4 4.3 multiply_reduce_fusion.19
  769.2 3.7 fusion.147
  775.0 4.3 multiply_reduce_fusion.19
  795.3 3.7 fusion.147
  801.1 4.3 multiply_reduce_fusion.19
  833.7 5.6 convolution_convert_fusion
  841.0 9.8 fusion.90
  851.8 11.4 fusion.47
  864.8 8.7 fusion.89
  873.6 42.2 %all-reduce.6 = (f32[4096]{0:T(1024)S(1)}, f32[4096]{0:T(1024)S(1)}, f32[1024]{0:T(1024)}, f32[1024]{0:T(1024)}) all-reduce(f32[4096]{0:T(1024)S(1)} %get-tuple-element.280, f32[4096]{0:T(1024)S(1)} %get-tuple-element.279, f32[1024]{0:T(1024)S(1)} %get-tuple-element.283, ...), channel_id=7, replica_groups=mesh['dp'=2,'head'=16] {'dp','head'}, use_global_device_ids=true, to_apply=%region_35.36.clone | all-reduce | flops 10240 | bytes 81920
  917.0 5.1 psum.52
  929.1 14.2 reduce-scatter.8.cloned.1.call-done
  945.4 184.3 %reduce-scatter.14.cloned.1.call-done = f32[128,1024]{1,0:T(8,128)} async-done(((f32[4096,1024]{1,0:T(8,128)}), f32[128,1024]{1,0:T(8,128)}) %reduce-scatter.14.cloned.1.call-update) | async-done | bytes 524304 | tf_op jit(solution)/shard_map/reduce_scatter | solution.py:276
  1129.7 187.4 %reduce-scatter.12.cloned.1.call-done = f32[128,1024]{1,0:T(8,128)} async-done(((f32[4096,1024]{1,0:T(8,128)}), f32[128,1024]{1,0:T(8,128)}) %reduce-scatter.12.cloned.1.call-update) | async-done | bytes 524304 | tf_op jit(solution)/shard_map/reduce_scatter | solution.py:275
  1317.1 187.7 %reduce-scatter.10.cloned.1.call-done = f32[128,1024]{1,0:T(8,128)} async-done(((f32[4096,1024]{1,0:T(8,128)}), f32[128,1024]{1,0:T(8,128)}) %reduce-scatter.10.cloned.1.call-update) | async-done | bytes 524304 | tf_op jit(solution)/shard_map/reduce_scatter | solution.py:274
  (451 shorter events, 206.2 us)
Async XLA Ops:
  8.0 150.9 %copy-start = (bf16[64,1024]{1,0:T(8,128)(2,1)S(1)}, bf16[64,1024]{1,0:T(8,128)(2,1)}, u32[]{:S(2)}) copy-start(bf16[64,1024]{1,0:T(8,128)(2,1)} %param.25) | copy-start | bytes 393220
  8.0 80.6 %all-gather.8.cloned.1.call-start = ((), (), s32[]{:S(2)}) async-start(), calls=%async_computation.5 | async-start | bytes 8912896 | tf_op jit(solution)/shard_map/all_gather | solution.py:125
  8.8 371.4 %reduce-scatter.6.cloned.1.call-start = ((), (), s32[]{:S(2)}) async-start(), calls=%async_computation.6 | async-start | bytes 17825792 | tf_op jit(solution)/shard_map/reduce_scatter | solution.py:166
  9.7 86.3 %copy-start.46 = (f32[32]{0:T(128)}, f32[32]{0:T(128)S(1)}, u32[]{:S(2)}) copy-start(f32[32]{0:T(128)S(1)} %multiply_exponential_fusion) | copy-start | bytes 388
  12.6 82.4 %copy-start.32 = (bf16[1024,192]{0,1:T(8,128)(2,1)}, bf16[1024,192]{0,1:T(8,128)(2,1)S(1)}, u32[]{:S(2)}) copy-start(bf16[1024,192]{0,1:T(8,128)(2,1)S(1)} %constant_dynamic-update-slice_fusion.1) | copy-start | bytes 1179652
  13.4 82.6 %copy-start.36 = (f32[4096]{0:T(1024)}, f32[4096]{0:T(1024)S(1)}, u32[]{:S(2)}) copy-start(f32[4096]{0:T(1024)S(1)} %subtract_convert_fusion) | copy-start | bytes 49156
  98.4 428.6 %copy-start.12 = (f32[4096,1,32]{0,2,1:T(8,128)}, f32[4096,1,32]{0,2,1:T(8,128)S(1)}, u32[]{:S(2)}) copy-start(f32[4096,1,32]{0,2,1:T(8,128)S(1)} %get-tuple-element.365) | copy-start | bytes 1572868
  98.4 429.5 %copy-start.10 = (f32[4096,1,32]{0,2,1:T(8,128)}, f32[4096,1,32]{0,2,1:T(8,128)S(1)}, u32[]{:S(2)}) copy-start(f32[4096,1,32]{0,2,1:T(8,128)S(1)} %get-tuple-element.364) | copy-start | bytes 1572868
  167.1 40.5 %copy-start.49 = (bf16[128]{0:T(256)(128)(2,1)S(1)}, bf16[128]{0:T(256)(128)(2,1)}, u32[]{:S(2)}) copy-start(bf16[128]{0:T(256)(128)(2,1)} %param.29) | copy-start | bytes 772
  167.1 214.5 %copy-start.26 = (bf16[256,1024]{1,0:T(8,128)(2,1)S(1)}, bf16[256,1024]{1,0:T(8,128)(2,1)}, u32[]{:S(2)}) copy-start(bf16[256,1024]{1,0:T(8,128)(2,1)} %param.19) | copy-start | bytes 1572868
  167.1 214.5 %copy-start.42 = (f32[1024]{0:T(1024)S(1)}, f32[1024]{0:T(1024)}, u32[]{:S(2)}) copy-start(f32[1024]{0:T(1024)} %param.31) | copy-start | bytes 12292
  167.1 216.3 %all-gather.12.cloned.1.call-start = ((), (), s32[]{:S(2)}) async-start(), calls=%async_computation.8 | async-start | bytes 8650752 | tf_op jit(solution)/shard_map/all_gather | solution.py:172
  167.7 249.0 %all-gather.10.cloned.1.call-start = ((), (), s32[]{:S(2)}) async-start(), calls=%async_computation.7 | async-start | bytes 8650752 | tf_op jit(solution)/shard_map/all_gather | solution.py:171
  168.3 327.1 %all-gather.14.cloned.1.call-start = ((), (), s32[]{:S(2)}) async-start(), calls=%async_computation.9 | async-start | bytes 8650752 | tf_op jit(solution)/shard_map/all_gather | solution.py:173
  168.8 431.8 %all-gather.16.cloned.1.call-start = ((), (), s32[]{:S(2)}) async-start(), calls=%async_computation.10 | async-start | bytes 8912896 | tf_op jit(solution)/shard_map/all_gather | solution.py:202
  383.4 33.3 %copy-start.24 = (bf16[256,1024]{1,0:T(8,128)(2,1)}, bf16[256,1024]{1,0:T(8,128)(2,1)S(1)}, u32[]{:S(2)}) copy-start(bf16[256,1024]{1,0:T(8,128)(2,1)S(1)} %multiply_convert_fusion.7) | copy-start | bytes 1572868
  495.3 6.5 copy-start.23
  495.3 6.5 copy-start.43
  503.1 18.5 %slice-start.4 = ((s8[8388608]{0:T(1024)(128)(4,1)}), s8[4194304]{0:T(1024)(128)(4,1)S(1)}, s32[]{:S(2)}) async-start(s8[8388608]{0:T(1024)(128)(4,1)} %bitcast.208), calls=%async_computation.20 | async-start | bytes 8388608
  504.4 9.0 copy-start.30
  504.8 16.8 %slice-start.5 = ((s8[8388608]{0:T(1024)(128)(4,1)}), s8[4194304]{0:T(1024)(128)(4,1)S(1)}, s32[]{:S(2)}) async-start(s8[8388608]{0:T(1024)(128)(4,1)} %bitcast.208), calls=%async_computation.21 | async-start | bytes 8388608
  513.4 8.2 copy-start.28
  513.4 8.2 copy-start.22
  526.9 395.7 %all-reduce.10.cloned.1.call-start = ((), (), s32[]{:S(2)}) async-start(), calls=%async_computation.15 | async-start | bytes 1048576 | tf_op jit(solution)/shard_map/psum | solution.py:265
  609.6 209.0 %copy-start.35 = (f32[4096]{0:T(1024)S(1)}, f32[4096]{0:T(1024)}, u32[]{:S(2)}) copy-start(f32[4096]{0:T(1024)} %copy-done.34) | copy-start | bytes 49156
  609.6 209.0 %copy-start.45 = (f32[64]{0:T(128)S(1)}, f32[64]{0:T(128)}, u32[]{:S(2)}) copy-start(f32[64]{0:T(128)} %param.24) | copy-start | bytes 772
  609.6 211.0 %copy-start.41 = (f32[4096]{0:T(1024)S(1)}, f32[4096]{0:T(1024)}, u32[]{:S(2)}) copy-start(f32[4096]{0:T(1024)} %copy-done.40) | copy-start | bytes 49156
  628.6 5.3 copy-start.6
  654.6 5.3 copy-start.6
  680.5 5.3 copy-start.6
  706.5 5.3 copy-start.6
  732.4 5.3 copy-start.6
  759.4 5.3 copy-start.6
  785.9 5.3 copy-start.6
  811.6 5.3 copy-start.6
  818.6 5.8 copy-start.8
  818.6 5.8 copy-start.5
  818.6 5.9 copy-start.11
  818.6 5.9 copy-start.13
  818.6 5.9 copy-start.15
  818.6 5.9 copy-start.17
  820.7 6.9 slice-start.2
  833.4 110.0 %reduce-scatter.8.cloned.1.call-start = ((), (), s32[]{:S(2)}) async-start(), calls=%async_computation.11 | async-start | bytes 8912896 | tf_op jit(solution)/shard_map/reduce_scatter | solution.py:258
  839.4 290.3 %reduce-scatter.14.cloned.1.call-start = ((), (), s32[]{:S(2)}) async-start(), calls=%async_computation.14 | async-start | bytes 17301504 | tf_op jit(solution)/shard_map/reduce_scatter | solution.py:276
  850.8 466.3 %reduce-scatter.12.cloned.1.call-start = ((), (), s32[]{:S(2)}) async-start(), calls=%async_computation.13 | async-start | bytes 17301504 | tf_op jit(solution)/shard_map/reduce_scatter | solution.py:275
  863.3 641.6 %reduce-scatter.10.cloned.1.call-start = ((), (), s32[]{:S(2)}) async-start(), calls=%async_computation.12 | async-start | bytes 17301504 | tf_op jit(solution)/shard_map/reduce_scatter | solution.py:274
  873.5 69.9 %copy-start.19 = (f32[256,1024]{1,0:T(8,128)S(1)}, f32[256,1024]{1,0:T(8,128)}, u32[]{:S(2)}) copy-start(f32[256,1024]{1,0:T(8,128)} %copy-done.18) | copy-start | bytes 3145732
  873.5 631.3 %copy-start.1 = (bf16[64,1024]{1,0:T(8,128)(2,1)S(1)}, bf16[64,1024]{1,0:T(8,128)(2,1)}, u32[]{:S(2)}) copy-start(bf16[64,1024]{1,0:T(8,128)(2,1)} %param.25) | copy-start | bytes 393220
  (55 other events, 122.4 us)
Sparse Core Ops, SparseCore 0:
  11.0 77.5 all-gather.7
  167.2 212.8 reduce-scatter.5
  527.0 73.5 all-gather.15
  839.5 103.8 reduce-scatter.7
  946.2 183.4 reduce-scatter.13
  1132.5 184.5 reduce-scatter.11
  1320.1 184.7 reduce-scatter.9
Sparse Core Ops, SparseCore 1:
  170.4 126.6 all-gather.11
  299.8 116.8 all-gather.9
  419.5 75.8 all-gather.13
  833.5 27.2 all-reduce.9
where the time goes:
time: 1520 us; the launch traced here: 1510 us
  waiting for transfers between devices  951 us (63%)
  matrix products  256 us (17%)
  blocking collectives  124 us (8%)
  local copies, waits for them, and re-layouts  87.1 us (6%)
  other arithmetic  38.9 us (3%)
  loops' own time  37.7 us (2%)
  between operations  17 us (1%)
    reduce_scatter x1, waiting for transfers between devices, shards(): lax.psum_scatter(up_grad, ('dp', 'head'), scatter_dimension=0, tiled=True)  188 us
    reduce_scatter x1, waiting for transfers between devices, shards(): lax.psum_scatter(gate_grad, ('dp', 'head'), scatter_dimension=0, tiled=True)  187 us
    reduce_scatter x1, waiting for transfers between devices, shards(): lax.psum_scatter(down_grad, ('dp', 'head'), scatter_dimension=0, tiled=True)  184 us
    reduce_scatter x1, waiting for transfers between devices, shards(): lax.psum_scatter(product(head_out, w_out), 'head', scatter_dimension=0, t...  134 us
    all_gather x1, waiting for transfers between devices, shards(): group_tokens = lax.all_gather(tokens, 'head', axis=0, tiled=True)  75.3 us
    all_gather x1, waiting for transfers between devices, shards(): group_branch = lax.all_gather(branch_low, 'head', axis=0, tiled=True)  71.9 us
    all_gather x1, waiting for transfers between devices, shards(): lax.all_gather(down_weight, ('dp', 'head'), axis=0, tiled=True)  68.4 us
    dot_general x16, matrix products, block_scores(): jnp.einsum('qhd,khd->hqk', query_rows, key_rows, preferred_element_type=j...  52.5 us
  transfers between devices with their start and end apart: 11, of which 9 were waited for; matrix products, arithmetic and copies ran while one was open for 5% of the time, Pallas kernels for 0%

commit v1 on v0

v1 whole, which is shorter than its diff:
```python
import math

import jax
import jax.numpy as jnp
from jax import lax
from jax.experimental import pallas as pl
from jax.experimental.pallas import tpu as pltpu
from jax.sharding import Mesh
from jax.sharding import PartitionSpec as P

HEAD_DIM = 64
BLOCK = 512
EPSILON = 1e-06
ROOT = math.sqrt(HEAD_DIM)
SCORE_SCALE = math.log2(math.e) / ROOT
AXES = ("o", "x", "z", "y", "c")
GROUP = ("z", "y", "c")
PLANE = ("x", "y", "c")
OWNERS = ("o", "z")
f32, bf16 = jnp.float32, jnp.bfloat16
VMEM_LIMIT = 56 * 2**20


def dot(left, right, left_dim, right_dim):
    return lax.dot_general(
        left, right, (((left_dim,), (right_dim,)), ((), ())), preferred_element_type=f32
    )


def unit_start(lengths, unit):
    start, end = jnp.int32(0), jnp.int32(0)
    for j in range(lengths.shape[1]):
        end = end + lengths[0, j]
        start = jnp.where(unit >= end, end, start)
    return start


def causal(weights):
    key = lax.broadcasted_iota(jnp.int32, weights.shape, 0)
    query = lax.broadcasted_iota(jnp.int32, weights.shape, 1)
    return jnp.where(key <= query, weights, 0.0)


def block_columns(index):
    return pl.ds(pl.multiple_of(index * BLOCK, BLOCK), BLOCK)


def attention_forward_kernel(lengths, qt, kt, vt, ot, lse):
    def unit(u, _):
        columns = block_columns(u)
        query = qt[:, columns]

        def part(j, carry, diagonal):
            total, attended = carry
            keys = block_columns(j)
            weights = jnp.exp2(dot(kt[:, keys], query, 0, 0) * SCORE_SCALE)
            if diagonal:
                weights = causal(weights)
            total = total + jnp.sum(weights, axis=0, keepdims=True)
            attended = attended + dot(vt[:, keys], weights.astype(bf16), 1, 0)
            return total, attended

        carry = (jnp.zeros((1, BLOCK), f32), jnp.zeros((HEAD_DIM, BLOCK), f32))
        carry = lax.fori_loop(unit_start(lengths, u), u, lambda j, c: part(j, c, False), carry)
        total, attended = part(u, carry, True)
        ot[:, columns] = (attended * (1.0 / total)).astype(bf16)
        lse[:, columns] = jnp.log2(total)
        return 0

    lax.fori_loop(0, qt.shape[1] // BLOCK, unit, 0)


def attention_backward_kernel(lengths, qt, kt, vt, ot, got, lse, gqt, gkt, gvt):
    def unit(u, _):
        columns = block_columns(u)
        query, grad, log_total = qt[:, columns], got[:, columns], lse[:, columns]
        inner = jnp.sum(grad.astype(f32) * ot[:, columns].astype(f32), axis=0, keepdims=True)

        def part(j, query_grad, diagonal):
            keys = block_columns(j)
            key, value = kt[:, keys], vt[:, keys]
            weights = jnp.exp2(dot(key, query, 0, 0) * SCORE_SCALE - log_total)
            if diagonal:
                weights = causal(weights)
            weight_grad = dot(value, grad, 0, 0)
            score_grad = (weights * (weight_grad - inner)).astype(bf16)
            key_part = dot(query, score_grad, 1, 1)
            value_part = dot(grad, weights.astype(bf16), 1, 1)
            if diagonal:
                gkt[:, keys] = key_part
                gvt[:, keys] = value_part
            else:
                gkt[:, keys] += key_part
                gvt[:, keys] += value_part
            return query_grad + dot(key, score_grad, 1, 0)

        query_grad = part(u, jnp.zeros((HEAD_DIM, BLOCK), f32), True)
        gqt[:, columns] = lax.fori_loop(
            unit_start(lengths, u), u, lambda j, c: part(j, c, False), query_grad
        )
        return 0

    lax.fori_loop(0, qt.shape[1] // BLOCK, unit, 0)


def attention_call(kernel, name, outs, lengths, *operands):
    vmem = pl.BlockSpec(memory_space=pltpu.VMEM)
    return pl.pallas_call(
        kernel,
        name=name,
        out_shape=outs,
        in_specs=[pl.BlockSpec(memory_space=pltpu.SMEM)] + [vmem] * len(operands),
        out_specs=tuple(vmem for _ in outs),
        compiler_params=pltpu.CompilerParams(vmem_limit_bytes=VMEM_LIMIT),
    )(lengths, *operands)


def attention_forward(lengths, qt, kt, vt):
    rows = qt.shape[1]
    outs = (jax.ShapeDtypeStruct((HEAD_DIM, rows), bf16), jax.ShapeDtypeStruct((1, rows), f32))
    return attention_call(attention_forward_kernel, "attn_forward", outs, lengths, qt, kt, vt)


def attention_backward(lengths, *operands):
    outs = (jax.ShapeDtypeStruct(operands[0].shape, f32),) * 3
    return attention_call(attention_backward_kernel, "attn_backward", outs, lengths, *operands)


def sphere(values):
    return values * lax.rsqrt(jnp.mean(values * values, axis=-1, keepdims=True) + EPSILON)


def turn_table(lengths_row, rows):
    ends = jnp.sum(jnp.where(jnp.tri(lengths_row.shape[0], dtype=bool), lengths_row[None, :], 0), 1)
    row = jnp.arange(rows, dtype=jnp.int32)
    passed = (row // BLOCK)[None, :] >= ends[:, None]
    place = row - BLOCK * jnp.max(jnp.where(passed, ends[:, None], 0), axis=0)
    half = HEAD_DIM // 2
    frequency = jnp.exp(jnp.arange(half, dtype=f32) * (-2.0 * math.log(10000.0) / HEAD_DIM))
    angle = place.astype(f32)[None, :] * frequency[:, None]
    return jnp.cos(angle), jnp.sin(angle)


def turn(values, cosine, sine):
    half = HEAD_DIM // 2
    a, b = values[:half], values[half:]
    return jnp.concatenate([a * cosine - b * sine, b * cosine + a * sine], axis=0)


def unit_features(turned):
    scale = lax.rsqrt(jnp.mean(turned * turned, axis=0, keepdims=True) + EPSILON)
    return turned * scale, scale


def features_back(turned, gain, grad, cosine, sine):
    normal, scale = unit_features(turned)
    gain_grad = jnp.sum(grad * normal, axis=1)
    grad = grad * gain[:, None]
    grad = scale * (grad - normal * jnp.mean(grad * normal, axis=0, keepdims=True))
    return turn(grad, cosine, -sine), gain_grad


def front(branch, own_tokens, alpha):
    return sphere(own_tokens + alpha * (sphere(branch) - own_tokens))


def core(up_proj, gate_proj, up_scale, gate_scale):
    gated = gate_proj * gate_scale
    return up_proj * up_scale * (gated * jax.nn.sigmoid(gated))


def gather(values, axes):
    return lax.all_gather(values, axes, axis=0, tiled=True)


def scatter_sum(values, axes):
    return lax.psum_scatter(values, axes, scatter_dimension=0, tiled=True)


def shards(
    tokens, lengths, w_query, w_key, w_value, s_qk, w_out, up_weight, gate_weight, down_weight,
    s_up, s_gate, alpha_attn, alpha_mlp, cotangent,
):
    units = up_weight.shape[0]
    mlp_weight = gather(jnp.stack([up_weight, gate_weight, down_weight])[None], OWNERS)
    mlp_scale = gather(jnp.stack([s_up, s_gate])[None], OWNERS).astype(f32)
    owners = mlp_weight.shape[0]
    up_full, gate_full, down_full = (
        mlp_weight[:, i].reshape(owners * units, -1) for i in range(3)
    )
    up_scale, gate_scale = (mlp_scale[:, i].reshape(1, owners * units) for i in range(2))

    group_tokens = gather(tokens, GROUP)
    rows = group_tokens.shape[0]
    cosine, sine = turn_table(lengths[0], rows)
    joint = jnp.concatenate([w_query, w_key, w_value], axis=1)
    projected = dot(joint, group_tokens, 0, 1)
    gain = s_qk[:, None]
    turned_q = turn(projected[:HEAD_DIM], cosine, sine)
    turned_k = turn(projected[HEAD_DIM : 2 * HEAD_DIM], cosine, sine)
    qt = (unit_features(turned_q)[0] * gain).astype(bf16)
    kt = (unit_features(turned_k)[0] * gain).astype(bf16)
    vt = projected[2 * HEAD_DIM :].astype(bf16)
    ot, lse = attention_forward(lengths, qt, kt, vt)
    branch = scatter_sum(dot(ot, w_out, 0, 0).astype(bf16), GROUP).astype(f32)

    hidden, front_pull = jax.vjp(front, branch, tokens.astype(f32), alpha_attn)
    hidden_low = gather(hidden.astype(bf16), PLANE)
    up_proj = dot(hidden_low, up_full, 1, 1)
    gate_proj = dot(hidden_low, gate_full, 1, 1)
    inner, core_pull = jax.vjp(core, up_proj, gate_proj, up_scale, gate_scale)
    inner_low = inner.astype(bf16)
    mlp_out = scatter_sum(dot(inner_low, down_full, 1, 0).astype(bf16), PLANE).astype(f32)
    mixed, finish_pull = jax.vjp(front, mlp_out, hidden, alpha_mlp)
    mlp_out_grad, hidden_grad, alpha_mlp_grad = finish_pull(cotangent.astype(f32))
    mlp_out_low = gather(mlp_out_grad.astype(bf16), PLANE)
    down_grad = dot(inner_low, mlp_out_low, 0, 0)
    up_proj_grad, gate_proj_grad, up_scale_grad, gate_scale_grad = core_pull(
        dot(mlp_out_low, down_full, 1, 1)
    )
    up_low, gate_low = up_proj_grad.astype(bf16), gate_proj_grad.astype(bf16)
    hidden_part = dot(up_low, up_full, 1, 0) + dot(gate_low, gate_full, 1, 0)
    hidden_grad = hidden_grad + scatter_sum(hidden_part.astype(bf16), PLANE).astype(f32)
    up_grad = dot(up_low, hidden_low, 0, 0)
    gate_grad = dot(gate_low, hidden_low, 0, 0)
    mlp_grads = jnp.stack(
        [g.astype(bf16).reshape(owners, units, -1) for g in (up_grad, gate_grad, down_grad)], 1
    )
    mlp_grads = scatter_sum(mlp_grads, OWNERS)[0].astype(f32)
    scale_grads = jnp.stack(
        [g.reshape(owners, units) for g in (up_scale_grad, gate_scale_grad)], axis=1
    )
    scale_grads = scatter_sum(scale_grads, OWNERS)[0]
    branch_grad, token_grad, alpha_attn_grad = front_pull(hidden_grad)

    group_branch = gather(branch_grad.astype(bf16), GROUP)
    got = dot(w_out, group_branch, 1, 1).astype(bf16)
    out_grad = dot(ot, group_branch, 1, 0)
    gqt, gkt, gvt = attention_backward(lengths, qt, kt, vt, ot, got, lse)
    gqt, query_gain_grad = features_back(turned_q, s_qk, gqt * (1.0 / ROOT), cosine, sine)
    gkt, key_gain_grad = features_back(turned_k, s_qk, gkt * (1.0 / ROOT), cosine, sine)
    joint_grad = jnp.concatenate([gqt, gkt, gvt], axis=0).astype(bf16)
    token_part = dot(joint_grad, joint, 0, 1)
    token_attn_grad = scatter_sum(token_part.astype(bf16), GROUP).astype(f32)
    joint_weight_grad = dot(group_tokens, joint_grad, 0, 1)
    dp = ("o", "x")
    joint_weight_grad = lax.psum(joint_weight_grad.astype(bf16), dp).astype(f32)
    out_grad = lax.psum(out_grad.astype(bf16), dp).astype(f32)
    gain_grad = lax.psum(query_gain_grad + key_gain_grad, dp)
    alpha_sums = lax.psum(jnp.stack([alpha_attn_grad, alpha_mlp_grad]), AXES)
    return (
        mixed.astype(bf16),
        (token_grad + token_attn_grad).astype(bf16),
        joint_weight_grad[:, :HEAD_DIM],
        joint_weight_grad[:, HEAD_DIM : 2 * HEAD_DIM],
        joint_weight_grad[:, 2 * HEAD_DIM :],
        gain_grad,
        out_grad,
        mlp_grads[0],
        mlp_grads[1],
        mlp_grads[2],
        scale_grads[0],
        scale_grads[1],
        alpha_sums[0],
        alpha_sums[1],
    )


def solution(mesh):
    dp, head = mesh.shape["dp"], mesh.shape["head"]
    fine = Mesh(mesh.devices.reshape(dp // 2, 2, head // 4, 2, 2), AXES)
    group, rows, heads = P(("o", "x"), None), P(AXES, None), P(None, GROUP)
    in_specs = (
        rows, group, heads, heads, heads, P(GROUP), P(GROUP, None), rows, rows, rows,
        P(AXES), P(AXES), P(), P(), rows,
    )
    out_specs = (
        rows, rows, heads, heads, heads, P(GROUP), P(GROUP, None), rows, rows, rows,
        P(AXES), P(AXES), P(), P(),
    )
    return jax.shard_map(
        shards, mesh=fine, in_specs=in_specs, out_specs=out_specs, check_vma=False
    )
```

time: 1520 us -> 786 us (0.52)
  waiting for transfers between devices: 951 us -> 538 us
  matrix products: 256 us -> 74.8 us
  local copies, waits for them, and re-layouts: 87.1 us -> 17.4 us
  blocking collectives: 124 us -> 64.6 us
  loops' own time: 37.7 us -> 0 us
  Pallas kernels: 0 us -> 26 us
    reduce_scatter x5, waiting for transfers between devices: 708 us -> 299 us  [scatter_sum(): return lax.psum_scatter(values, axes, scatter_dimension=0, tiled=True)]
    dot_general x71 -> x15, matrix products: 256 us -> 74.8 us  [dot(): lax.dot_general(left, right, (((left_dim,), (right_dim,)), ((), ())), pre...]
    all_gather x2 -> x1, blocking collectives: 76.9 us -> 9.88 us  [gather(): return lax.all_gather(values, axes, axis=0, tiled=True)]
    psum x1 -> x2, blocking collectives: 5.11 us -> 45 us  [the longest x1 39.3 us: shards(): alpha_sums = lax.psum(jnp.stack([alpha_attn_grad, alpha_mlp_grad]), AXES)]
    another operation x2 -> x0, loops' own time: 37.7 us -> none  [the longest x1 26.9 us: shards(): lax.scan(backward_block, (zeros_heads, zeros_heads), jnp.arange(blocks, d...]
    dynamic_update_slice x24 -> x0, local copies, waits for them, and re-layouts: 35.3 us -> none  [the longest x8 26.5 us: backward_block(): lax.dynamic_update_slice_in_dim(key_acc, lax.dynamic_slice_in_dim(key_acc...]
    unnamed x1, blocking collectives: 42.2 us -> 9.71 us
    pallas_call x0 -> x2, Pallas kernels: none -> 26 us  [attention_call(): pl.pallas_call(kernel, name=name, out_shape=outs, in_specs=[pl.BlockSpec(...]
  transfers between devices with their start and end apart: 11 -> 11, of which waited for: 9 -> 8; matrix products, arithmetic and copies ran while one was open for 5% -> 9% of each run, Pallas kernels for 0% -> 2%
where the time goes in v1:
time: 786 us; the launch traced here: 779 us
  waiting for transfers between devices  538 us (68%)
  matrix products  74.8 us (10%)
  blocking collectives  64.6 us (8%)
  other arithmetic  41.7 us (5%)
  Pallas kernels  26 us (3%)
  local copies, waits for them, and re-layouts  17.4 us (2%)
  between operations  16.1 us (2%)
    reduce_scatter x5, waiting for transfers between devices, scatter_sum(): return lax.psum_scatter(values, axes, scatter_dimension=0, tiled=True)  299 us
    all_gather x5, waiting for transfers between devices, gather(): return lax.all_gather(values, axes, axis=0, tiled=True)  238 us
    dot_general x15, matrix products, dot(): lax.dot_general(left, right, (((left_dim,), (right_dim,)), ((), ())), pre...  74.8 us
    psum x1, blocking collectives, shards(): alpha_sums = lax.psum(jnp.stack([alpha_attn_grad, alpha_mlp_grad]), AXES)  39.3 us
    pallas_call x2, Pallas kernels, attention_call(): pl.pallas_call(kernel, name=name, out_shape=outs, in_specs=[pl.BlockSpec(...  26 us
  transfers between devices with their start and end apart: 11, of which 8 were waited for; matrix products, arithmetic and copies ran while one was open for 9% of the time, Pallas kernels for 2%

profile of v1, /device:TPU:0, one launch (start us, length us, event | category | flops | bytes accessed | tf_op | source)
XLA Modules:
  0.0 779.4 jit_solution(3298086372677788378)
XLA Ops:
  12.5 76.1 %all-gather.9.cloned.1.call-done = bf16[4096,1024]{1,0:T(8,128)(2,1)} async-done(((bf16[256,1024]{1,0:T(8,128)(2,1)}), bf16[4096,1024]{1,0:T(8,128)(2,1)}) %all-gather.9.cloned.1.call-update) | async-done | bytes 8388624 | tf_op jit(solution)/shard_map/all_gather | solution.py:173
  88.7 6.3 fusion.60
  95.8 2.4 fusion.42
  100.2 9.4 %attn_forward.1 = (bf16[64,4096]{1,0:T(8,128)(2,1)}, f32[1,4096]{1,0:T(1,128)}) custom-call(s32[1,4]{1,0:T(1,128)} %lengths.3, bf16[64,4096]{1,0:T(8,128)(2,1)} %get-tuple-element.71.qt, bf16[64,4096]{1,0:T(8,128)(2,1)} %get-tuple-element.70.kt, bf16[64,4096]{1,0:T(8,128)(2,1)} %slice.168.vt), custom_call_target="tpu_custom_call" | custom-call | tf_op jit(solution)/shard_map/attn_forward/pallas_call | solution.py:108
  109.7 6.7 convolution_convert_fusion.1
  118.5 129.6 %reduce-scatter.6.cloned.1.call-done = bf16[256,1024]{1,0:T(8,128)(2,1)} async-done(((bf16[4096,1024]{1,0:T(8,128)(2,1)}), bf16[256,1024]{1,0:T(8,128)(2,1)}) %reduce-scatter.6.cloned.1.call-update) | async-done | bytes 524304 | tf_op jit(solution)/shard_map/reduce_scatter | solution.py:177
  249.3 1.5 multiply_reduce_fusion.10
  250.9 2.3 multiply_convert_fusion.6
  253.3 9.9 %all-gather.2 = bf16[4,2,128]{2,1,0:T(2,128)(2,1)S(1)} all-gather(bf16[1,2,128]{2,1,0:T(2,128)(2,1)S(1)} %maximum_bitcast_fusion), channel_id=3, replica_groups=mesh['o'=1,'x'=2,'z'=4,'y'=2,'c'=2] {'o','z'}, dimensions={0}, use_global_device_ids=true | all-gather | bytes 2560 | tf_op jit(solution)/shard_map/all_gather | solution.py:173
  263.1 3.6 fusion.56
  266.8 22.8 %all-gather.11.cloned.1.call-done = bf16[2048,1024]{1,0:T(8,128)(2,1)} async-done(((bf16[256,1024]{1,0:T(8,128)(2,1)}), bf16[2048,1024]{1,0:T(8,128)(2,1)}) %all-gather.11.cloned.1.call-update) | async-done | bytes 4194320 | tf_op jit(solution)/shard_map/all_gather | solution.py:173
  289.6 4.7 fusion.61
  294.4 5.2 multiply_convert_fusion.2
  299.6 1.3 copy-done.37
  300.9 4.3 convolution_convert_fusion.3
  305.3 51.3 %reduce-scatter.8.cloned.1.call-done = bf16[256,1024]{1,0:T(8,128)(2,1)} async-done(((bf16[2048,1024]{1,0:T(8,128)(2,1)}), bf16[256,1024]{1,0:T(8,128)(2,1)}) %reduce-scatter.8.cloned.1.call-update) | async-done | bytes 524304 | tf_op jit(solution)/shard_map/reduce_scatter | solution.py:177
  357.9 1.9 fusion.5
  359.8 2.4 fusion.12
  363.9 36.1 %all-gather.13.cloned.1.call-done = bf16[2048,1024]{1,0:T(8,128)(2,1)} async-done(((bf16[256,1024]{1,0:T(8,128)(2,1)}), bf16[2048,1024]{1,0:T(8,128)(2,1)}) %all-gather.13.cloned.1.call-update) | async-done | bytes 4194320 | tf_op jit(solution)/shard_map/all_gather | solution.py:173
  400.0 9.9 %multiply_reduce_fusion.1 = (f32[512]{0:T(512)S(1)}, f32[512]{0:T(512)S(1)}, f32[2048,512]{1,0:T(8,128)S(1)}, bf16[2048,512]{1,0:T(8,128)(2,1)S(1)}) fusion(f32[2048,512]{1,0:T(8,128)} %get-tuple-element.73, f32[2048,512]{1,0:T(8,128)} %copy-done.38, f32[512]{0:T(512)S(1)} %bitcast.90, f32[512]{0:T(512)S(1)} %bitcast.98, ...), kind=kOutput, calls=%fused_computation.9 | convolution fusion | flops 2168454144 | bytes 19931136 | tf_op jit(solution)/shard_map/dot_general | solution.py:25
  409.9 2.3 fusion.62
  412.5 4.4 add_convert_fusion
  417.0 51.3 %reduce-scatter.10.cloned.1.call-done = bf16[256,1024]{1,0:T(8,128)(2,1)} async-done(((bf16[2048,1024]{1,0:T(8,128)(2,1)}), bf16[256,1024]{1,0:T(8,128)(2,1)}) %reduce-scatter.10.cloned.1.call-update) | async-done | bytes 524304 | tf_op jit(solution)/shard_map/reduce_scatter | solution.py:177
  468.2 2.1 multiply_reduce_fusion.2
  470.3 2.0 multiply_reduce_fusion.3
  474.5 5.3 convolution_convert_fusion.4
  479.8 2.4 convolution_convert_fusion.6
  482.3 2.4 convolution_convert_fusion.5
  484.6 2.0 pad_maximum_fusion
  486.9 103.1 %all-gather.15.cloned.1.call-done = bf16[4096,1024]{1,0:T(8,128)(2,1)} async-done(((bf16[256,1024]{1,0:T(8,128)(2,1)}), bf16[4096,1024]{1,0:T(8,128)(2,1)}) %all-gather.15.cloned.1.call-update) | async-done | bytes 8388624 | tf_op jit(solution)/shard_map/all_gather | solution.py:173
  590.0 6.8 fusion.got
  596.9 16.5 %attn_backward.1 = (f32[64,4096]{1,0:T(8,128)}, f32[64,4096]{1,0:T(8,128)}, f32[64,4096]{1,0:T(8,128)}) custom-call(s32[1,4]{1,0:T(1,128)} %lengths.3, bf16[64,4096]{1,0:T(8,128)(2,1)} %get-tuple-element.71.qt, bf16[64,4096]{1,0:T(8,128)(2,1)} %get-tuple-element.70.kt, bf16[64,4096]{1,0:T(8,128)(2,1)} %slice.168.vt, bf16[64,4096]{1,0:T(8,128)(2,1)} %get-tuple-element.19.ot, ...), custom_call_target="tpu_custom_call" | custom-call | tf_op jit(solution)/shard_map/attn_backward/pallas_call | solution.py:108
  613.4 2.3 multiply_reduce_fusion.4
  615.8 5.8 convolution_convert_fusion.8
  622.1 2.3 fusion.47
  624.4 2.3 fusion.46
  626.6 2.3 fusion.45
  628.9 2.3 fusion.44
  631.3 2.6 fusion.4
  634.0 5.7 convolution_convert_fusion
  640.9 9.7 %all-reduce = f32[4,2,128]{2,1,0:T(2,128)S(1)} all-reduce(f32[4,2,128]{2,1,0:T(2,128)S(1)} %pad_maximum_fusion.5), channel_id=9, replica_groups=mesh['o'=1,'x'=2,'z'=4,'y'=2,'c'=2] {'o','z'}, use_global_device_ids=true, to_apply=%region_26.27.clone | all-reduce | flops 1024 | bytes 8192
  651.8 1.3 convert_element_type.137
  653.2 39.3 %psum.31 = f32[2,1024]{1,0:T(2,128)S(1)} all-reduce(f32[2,1024]{1,0:T(2,128)S(1)} %pad_maximum_fusion.4), channel_id=1, replica_groups=mesh['o'=1,'x'=2,'z'=4,'y'=2,'c'=2] {'o','x','z','y','c'}, use_global_device_ids=true, to_apply=%region_29.30 | all-reduce | flops 2048 | bytes 16384 | tf_op jit(solution)/shard_map/psum | solution.py:250
  694.3 5.7 psum.29
  699.9 1.6 convert_element_type.133
  701.6 1.9 fusion.57
  703.5 66.6 %reduce-scatter.12.cloned.1.call-done = bf16[256,1024]{1,0:T(8,128)(2,1)} async-done(((bf16[4096,1024]{1,0:T(8,128)(2,1)}), bf16[256,1024]{1,0:T(8,128)(2,1)}) %reduce-scatter.12.cloned.1.call-update) | async-done | bytes 524304 | tf_op jit(solution)/shard_map/reduce_scatter | solution.py:177
  770.0 2.0 add_convert_fusion.1
  (147 shorter events, 21.2 us)
Async XLA Ops:
  8.0 101.7 %copy-start = (bf16[64,1024]{1,0:T(8,128)(2,1)S(1)}, bf16[64,1024]{1,0:T(8,128)(2,1)}, u32[]{:S(2)}) copy-start(bf16[64,1024]{1,0:T(8,128)(2,1)} %param.21) | copy-start | bytes 393220
  8.0 80.6 %all-gather.9.cloned.1.call-start = ((), (), s32[]{:S(2)}) async-start(), calls=%async_computation.5 | async-start | bytes 8912896 | tf_op jit(solution)/shard_map/all_gather | solution.py:173
  8.8 239.3 %reduce-scatter.6.cloned.1.call-start = ((), (), s32[]{:S(2)}) async-start(), calls=%async_computation.6 | async-start | bytes 8912896 | tf_op jit(solution)/shard_map/reduce_scatter | solution.py:177
  12.4 82.6 %copy-start.17 = (bf16[1024,192]{0,1:T(8,128)(2,1)}, bf16[1024,192]{0,1:T(8,128)(2,1)S(1)}, u32[]{:S(2)}) copy-start(bf16[1024,192]{0,1:T(8,128)(2,1)S(1)} %constant_dynamic-update-slice_fusion) | copy-start | bytes 1179652
  94.9 4.0 copy-start.29
  98.2 2.0 copy-start.5
  116.4 1.0 copy-start.25
  116.4 1.1 copy-start.26
  116.4 133.0 %copy-start.2 = (bf16[256,1024]{1,0:T(8,128)(2,1)S(1)}, bf16[256,1024]{1,0:T(8,128)(2,1)}, u32[]{:S(2)}) copy-start(bf16[256,1024]{1,0:T(8,128)(2,1)} %param.15) | copy-start | bytes 1572868
  116.4 133.0 %copy-start.27 = (f32[1024]{0:T(1024)S(1)}, f32[1024]{0:T(1024)}, u32[]{:S(2)}) copy-start(f32[1024]{0:T(1024)} %param.27) | copy-start | bytes 12292
  116.4 136.8 %copy-start.32 = (bf16[128]{0:T(256)(128)(2,1)S(1)}, bf16[128]{0:T(256)(128)(2,1)}, u32[]{:S(2)}) copy-start(bf16[128]{0:T(256)(128)(2,1)} %param.26) | copy-start | bytes 772
  116.4 136.8 %copy-start.33 = (bf16[128]{0:T(256)(128)(2,1)S(1)}, bf16[128]{0:T(256)(128)(2,1)}, u32[]{:S(2)}) copy-start(bf16[128]{0:T(256)(128)(2,1)} %param.25) | copy-start | bytes 772
  116.4 146.7 %all-gather.17.cloned.1.call-start = ((), (), s32[]{:S(2)}) async-start(), calls=%async_computation.14 | async-start | bytes 3932160 | tf_op jit(solution)/shard_map/all_gather | solution.py:173
  118.5 171.1 %all-gather.11.cloned.1.call-start = ((), (), s32[]{:S(2)}) async-start(), calls=%async_computation.7 | async-start | bytes 4718592 | tf_op jit(solution)/shard_map/all_gather | solution.py:173
  253.2 103.4 %reduce-scatter.8.cloned.1.call-start = ((), (), s32[]{:S(2)}) async-start(), calls=%async_computation.8 | async-start | bytes 4718592 | tf_op jit(solution)/shard_map/reduce_scatter | solution.py:177
  266.8 27.6 %copy-start.15 = (bf16[4,1,128,1024]{3,2,1,0:T(8,128)(2,1)}, bf16[4,1,128,1024]{3,2,1,0:T(8,128)(2,1)S(1)}, u32[]{:S(2)}) copy-start(bf16[4,1,128,1024]{3,2,1,0:T(8,128)(2,1)S(1)} %get-tuple-element.49) | copy-start | bytes 3145732
  289.6 4.8 copy-start.21
  289.6 4.8 copy-start.30
  294.3 5.2 copy-start.38
  294.4 6.5 copy-start.23
  299.6 1.3 copy-start.37
  305.2 52.7 %copy-start.1 = (bf16[256,1024]{1,0:T(8,128)(2,1)S(1)}, bf16[256,1024]{1,0:T(8,128)(2,1)}, u32[]{:S(2)}) copy-start(bf16[256,1024]{1,0:T(8,128)(2,1)} %reduce-scatter.6.cloned.1.call-done) | copy-start | bytes 1572868
  305.2 52.7 %copy-start.19 = (bf16[256,1024]{1,0:T(8,128)(2,1)S(1)}, bf16[256,1024]{1,0:T(8,128)(2,1)}, u32[]{:S(2)}) copy-start(bf16[256,1024]{1,0:T(8,128)(2,1)} %param.29) | copy-start | bytes 1572868
  305.2 52.7 %copy-start.28 = (f32[1024]{0:T(1024)S(1)}, f32[1024]{0:T(1024)}, u32[]{:S(2)}) copy-start(f32[1024]{0:T(1024)} %param.28) | copy-start | bytes 12292
  305.2 94.8 %all-gather.13.cloned.1.call-start = ((), (), s32[]{:S(2)}) async-start(), calls=%async_computation.9 | async-start | bytes 4718592 | tf_op jit(solution)/shard_map/all_gather | solution.py:173
  356.5 5.7 copy-start.7
  363.4 104.8 %reduce-scatter.10.cloned.1.call-start = ((), (), s32[]{:S(2)}) async-start(), calls=%async_computation.10 | async-start | bytes 4718592 | tf_op jit(solution)/shard_map/reduce_scatter | solution.py:177
  400.0 9.9 %copy-start.22 = (bf16[4,1,128,1024]{3,2,1,0:T(8,128)(2,1)S(1)}, bf16[4,1,128,1024]{3,2,1,0:T(8,128)(2,1)}, u32[]{:S(2)}) copy-start(bf16[4,1,128,1024]{3,2,1,0:T(8,128)(2,1)} %get-tuple-element.50) | copy-start | bytes 3145732
  409.9 2.4 copy-start.35
  409.9 2.6 copy-start.11
  409.9 2.6 copy-start.16
  416.9 173.1 %all-gather.15.cloned.1.call-start = ((), (), s32[]{:S(2)}) async-start(), calls=%async_computation.11 | async-start | bytes 8912896 | tf_op jit(solution)/shard_map/all_gather | solution.py:173
  474.4 177.4 %reduce-scatter.14.cloned.1.call-start = ((), (), s32[]{:S(2)}) async-start(), calls=%async_computation.13 | async-start | bytes 3932160 | tf_op jit(solution)/shard_map/reduce_scatter | solution.py:177
  474.5 5.3 copy-start.31
  474.5 5.3 copy-start.36
  479.8 2.4 copy-start.12
  486.7 126.7 %copy-start.4 = (f32[32,4096]{1,0:T(8,128)S(1)}, f32[32,4096]{1,0:T(8,128)}, u32[]{:S(2)}) copy-start(f32[32,4096]{1,0:T(8,128)} %copy-done.3) | copy-start | bytes 1572868
  486.7 126.7 %copy-start.6 = (f32[32,4096]{1,0:T(8,128)S(1)}, f32[32,4096]{1,0:T(8,128)}, u32[]{:S(2)}) copy-start(f32[32,4096]{1,0:T(8,128)} %copy-done.5) | copy-start | bytes 1572868
  486.7 213.2 %all-reduce.4.cloned.1.call-start = ((), (), s32[]{:S(2)}) async-start(), calls=%async_computation.15 | async-start | bytes 1048576 | tf_op jit(solution)/shard_map/psum | solution.py:247
  596.9 18.9 %copy-start.8 = (bf16[64,4096]{1,0:T(8,128)(2,1)S(1)}, bf16[64,4096]{1,0:T(8,128)(2,1)}, u32[]{:S(2)}) copy-start(bf16[64,4096]{1,0:T(8,128)(2,1)} %get-tuple-element.19.ot) | copy-start | bytes 1572868
  613.4 17.8 %slice-start = ((s8[8388608]{0:T(1024)(128)(4,1)}), s8[4194304]{0:T(1024)(128)(4,1)S(1)}, s32[]{:S(2)}) async-start(s8[8388608]{0:T(1024)(128)(4,1)} %bitcast.72), calls=%async_computation.16 | async-start | bytes 8388608
  615.8 5.8 copy-start.13
  615.8 5.8 copy-start.14
  615.8 15.4 %slice-start.1 = ((s8[8388608]{0:T(1024)(128)(4,1)}), s8[4194304]{0:T(1024)(128)(4,1)S(1)}, s32[]{:S(2)}) async-start(s8[8388608]{0:T(1024)(128)(4,1)} %bitcast.72), calls=%async_computation.17 | async-start | bytes 8388608
  622.1 9.1 %copy-start.20 = (f32[64,4096]{1,0:T(8,128)S(1)}, f32[64,4096]{1,0:T(8,128)}, u32[]{:S(2)}) copy-start(f32[64,4096]{1,0:T(8,128)} %get-tuple-element.23) | copy-start | bytes 3145732
  631.3 2.7 copy-start.18
  633.9 136.1 %reduce-scatter.12.cloned.1.call-start = ((), (), s32[]{:S(2)}) async-start(), calls=%async_computation.12 | async-start | bytes 8912896 | tf_op jit(solution)/shard_map/reduce_scatter | solution.py:177
  639.7 130.3 %copy-start.10 = (f32[256,1024]{1,0:T(8,128)S(1)}, f32[256,1024]{1,0:T(8,128)}, u32[]{:S(2)}) copy-start(f32[256,1024]{1,0:T(8,128)} %copy-done.9) | copy-start | bytes 3145732
  (4 other events, 3.4 us)
Sparse Core Ops, SparseCore 0:
  11.0 77.5 all-gather.8
  116.5 131.5 reduce-scatter.5
  474.5 115.4 all-gather.14
Sparse Core Ops, SparseCore 1:
  118.5 73.2 all-gather.16
  253.2 36.3 all-gather.10
  305.3 51.2 reduce-scatter.7
  363.5 36.5 all-gather.12
  417.0 51.2 reduce-scatter.9
  486.8 79.0 reduce-scatter.13
  634.0 28.2 all-reduce.3
  666.8 103.2 reduce-scatter.11

commit v2 on v1

--- a/solution.py
+++ b/solution.py
@@ -1,3 +1,4 @@
+import functools
 import math
 
 import jax
@@ -177,32 +178,347 @@
     return lax.psum_scatter(values, axes, scatter_dimension=0, tiled=True)
 
 
+MESH_ID = pl.DeviceIdType.MESH
+
+
+def here(*names):
+    return tuple(lax.axis_index(name) for name in names)
+
+
+def greet(neighbours):
+    barrier = pltpu.get_barrier_semaphore()
+    count = jnp.int32(0)
+    for condition, device in neighbours:
+
+        @pl.when(condition)
+        def _():
+            pl.semaphore_signal(barrier, inc=1, device_id=device, device_id_type=MESH_ID)
+
+        count = count + jnp.where(condition, 1, 0)
+    pl.semaphore_wait(barrier, count)
+
+
+def remote(source, target, send, receive, device):
+    return pltpu.make_async_remote_copy(
+        src_ref=source,
+        dst_ref=target,
+        send_sem=send,
+        recv_sem=receive,
+        device_id=device,
+        device_id_type=MESH_ID,
+    )
+
+
+def line_order(z, length, step):
+    picked = jnp.int32(0)
+    for at in range(length):
+        order = sorted(range(length), key=lambda p: (abs(p - at), p if at < length // 2 else -p))
+        picked = jnp.where(z == at, order[step], picked)
+    return picked
+
+
+def group_neighbours(length):
+    z, y, c = here("z", "y", "c")
+    return [
+        (z > 0, {"z": z - 1}),
+        (z < length - 1, {"z": z + 1}),
+        (z >= 0, {"y": 1 - y}),
+        (z >= 0, {"c": 1 - c}),
+    ]
+
+
+def group_gather(length, own, held, send, receive, on_unit):
+    z, y, c = here("z", "y", "c")
+    rows = held.shape[1] // 2
+
+    def block(zz, yy, cc):
+        return held.at[zz * 2 + yy, pl.ds(pl.multiple_of(cc * rows, rows), rows)]
+
+    def copy(kind, zz, yy, cc, device):
+        at = block(zz, yy, cc)
+        number = (zz * 2 + yy) * 2 + cc
+        return remote(at, at, send.at[kind, number], receive.at[number], device)
+
+    def arrived(zz, yy, cc):
+        copy(3, zz, yy, cc, {"c": 1 - c}).wait_recv()
+
+    def passed_on(zz, act):
+        @pl.when((zz <= z) & (z < length - 1))
+        def _():
+            act(copy(0, zz, y, c, {"z": z + 1}))
+
+        @pl.when((zz >= z) & (z > 0))
+        def _():
+            act(copy(1, zz, y, c, {"z": z - 1}))
+
+        act(copy(2, zz, y, c, {"y": 1 - y}))
+        act(copy(3, zz, y, c, {"c": 1 - c}))
+
+    block(z, y, c)[...] = own[...]
+    order = [line_order(z, length, step) for step in range(length)]
+    for step in range(length + 1):
+        if step < length:
+            if step > 0:
+                arrived(order[step], y, c)
+            passed_on(order[step], lambda copy_: copy_.start())
+        if step > 0:
+            zz = order[step - 1]
+            arrived(zz, y, 1 - c)
+            on_unit(zz * 2 + y)
+            arrived(zz, 1 - y, c)
+            copy(3, zz, 1 - y, c, {"c": 1 - c}).start()
+            arrived(zz, 1 - y, 1 - c)
+            on_unit(zz * 2 + 1 - y)
+    for step in range(length):
+        passed_on(order[step], lambda copy_: copy_.wait_send())
+        copy(3, order[step], 1 - y, c, {"c": 1 - c}).wait_send()
+
+
+GATHER_SEMAPHORES = 4
+
+
+def gather_scratch(units, rows, width):
+    return [
+        pltpu.VMEM((units, 2 * rows, width), bf16),
+        pltpu.SemaphoreType.DMA((GATHER_SEMAPHORES, 2 * units)),
+        pltpu.SemaphoreType.DMA((2 * units,)),
+    ]
+
+
+def scatter_scratch(length, rows, width):
+    return [
+        pltpu.VMEM((2 * length, rows, width), f32),
+        pltpu.VMEM((2, 2 * length, rows, width), bf16),
+        pltpu.VMEM((2, length, rows, width), bf16),
+        pltpu.VMEM((3, length, rows, width), bf16),
+        pltpu.SemaphoreType.DMA((2, 2 * length)),
+        pltpu.SemaphoreType.DMA((2, length)),
+        pltpu.SemaphoreType.DMA((3, length)),
+    ]
+
+
+def group_scatter(length, produce, own, cross, across, along, cross_sem, across_sem, along_sem, between=None):
+    z, y, c = here("z", "y", "c")
+
+    def to_core(unit):
+        return remote(cross.at[0, unit], cross.at[1, unit], cross_sem.at[0, unit], cross_sem.at[1, unit], {"c": 1 - c})
+
+    def to_y(zz):
+        return remote(across.at[0, zz], across.at[1, zz], across_sem.at[0, zz], across_sem.at[1, zz], {"y": 1 - y})
+
+    def to_z(zz, slot, device):
+        return remote(along.at[0, zz], along.at[slot, zz], along_sem.at[0, zz], along_sem.at[slot, zz], device)
+
+    def from_z(zz, slot):
+        to_z(zz, slot, {"c": 1 - c}).wait_recv()
+        return along[slot, zz].astype(f32)
+
+    order = [line_order(z, length, length - 1 - step) for step in range(length)]
+
+    def first(zz):
+        for yy in (1 - y, y):
+            unit = zz * 2 + yy
+            cross[0, unit] = produce(unit, 1 - c).astype(bf16)
+            to_core(unit).start()
+        for yy in (1 - y, y):
+            unit = zz * 2 + yy
+            own[unit] = produce(unit, c)
+
+    def second(zz):
+        unit = zz * 2 + 1 - y
+        to_core(unit).wait_recv()
+        across[0, zz] = (own[unit] + cross[1, unit].astype(f32)).astype(bf16)
+        to_y(zz).start()
+
+    def third(zz, last):
+        unit = zz * 2 + y
+        to_core(unit).wait_recv()
+        own[unit] += cross[1, unit].astype(f32)
+        to_y(zz).wait_recv()
+        own[unit] += across[1, zz].astype(f32)
+
+        @pl.when((zz >= z) & (z > 0))
+        def _():
+            own[unit] += from_z(zz, 1)
+
+        @pl.when((zz <= z) & (z < length - 1))
+        def _():
+            own[unit] += from_z(zz, 2)
+
+        if last:
+            return own[unit]
+        along[0, zz] = own[unit].astype(bf16)
+
+        @pl.when(zz > z)
+        def _():
+            to_z(zz, 1, {"z": z + 1}).start()
+
+        @pl.when(zz < z)
+        def _():
+            to_z(zz, 2, {"z": z - 1}).start()
+
+        return None
+
+    total = None
+    for step in range(length + 2):
+        if step < length:
+            first(order[step])
+        if 1 <= step <= length:
+            second(order[step - 1])
+        if step == length and between is not None:
+            between()
+        if step >= 2:
+            total = third(order[step - 2], step == length + 1)
+    for step in range(length):
+        zz = order[step]
+        for yy in (0, 1):
+            to_core(zz * 2 + yy).wait_send()
+        to_y(zz).wait_send()
+        if step < length - 1:
+            to_z(zz, 1, {"c": 1 - c}).wait_send()
+    return total
+
+
+def remote_call(kernel, name, number, outs, out_specs, in_specs, scratch, *operands):
+    return pl.pallas_call(
+        kernel,
+        name=name,
+        out_shape=outs,
+        in_specs=in_specs,
+        out_specs=out_specs,
+        scratch_shapes=scratch,
+        compiler_params=pltpu.CompilerParams(
+            collective_id=number, has_side_effects=True, vmem_limit_bytes=VMEM_LIMIT
+        ),
+    )(*operands)
+
+
+IN_VMEM = pl.BlockSpec(memory_space=pltpu.VMEM)
+ANYWHERE = pl.BlockSpec(memory_space=pl.ANY)
+
+
+def like(shape, dtype):
+    return jax.ShapeDtypeStruct(shape, dtype)
+
+
+def project_kernel(
+    length, tokens, joint, gain, cosine, sine, gathered, turned_q, turned_k, qt, kt, vt,
+    held, send, receive, out_sem,
+):
+    greet(group_neighbours(length))
+
+    def on_unit(unit):
+        copy = pltpu.make_async_copy(held.at[unit], gathered.at[unit], out_sem.at[unit])
+        copy.start()
+        columns = block_columns(unit)
+        projected = dot(joint[...], held[unit], 1, 1)
+        for part, turned, features in ((0, turned_q, qt), (1, turned_k, kt)):
+            values = turn(
+                projected[part * HEAD_DIM : (part + 1) * HEAD_DIM], cosine[:, columns], sine[:, columns]
+            )
+            turned[:, columns] = values
+            features[:, columns] = (unit_features(values)[0] * gain[...]).astype(bf16)
+        vt[:, columns] = projected[2 * HEAD_DIM :].astype(bf16)
+
+    group_gather(length, tokens, held, send, receive, on_unit)
+    for unit in range(2 * length):
+        pltpu.make_async_copy(held.at[unit], gathered.at[unit], out_sem.at[unit]).wait()
+
+
+def project(length, tokens, joint, gain, cosine, sine):
+    rows, width = tokens.shape
+    units = 2 * length
+    total = units * 2 * rows
+    wide, narrow = like((HEAD_DIM, total), f32), like((HEAD_DIM, total), bf16)
+    return remote_call(
+        functools.partial(project_kernel, length), "project", 1,
+        (like((units, 2 * rows, width), bf16), wide, wide, narrow, narrow, narrow),
+        (ANYWHERE,) + (IN_VMEM,) * 5, [IN_VMEM] * 5,
+        gather_scratch(units, rows, width) + [pltpu.SemaphoreType.DMA((units,))],
+        tokens, joint, gain, cosine, sine,
+    )
+
+
+def half_columns(unit, half):
+    rows = BLOCK // 2
+    return pl.ds(pl.multiple_of(unit * BLOCK + half * rows, rows), rows)
+
+
+def branch_kernel(length, ot, w_out, branch, *scratch):
+    greet(group_neighbours(length))
+    branch[...] = group_scatter(
+        length, lambda unit, half: dot(ot[:, half_columns(unit, half)], w_out[...], 0, 0), *scratch
+    )
+
+
+def branch_sum(length, ot, w_out, rows):
+    width = w_out.shape[1]
+    return remote_call(
+        functools.partial(branch_kernel, length), "branch_sum", 2,
+        like((rows, width), f32), IN_VMEM, [IN_VMEM] * 2, scatter_scratch(length, rows, width), ot, w_out,
+    )
+
+
+def spread_kernel(length, grad, w_out, ot, got, out_grad, held, send, receive):
+    greet(group_neighbours(length))
+    out_grad[...] = jnp.zeros_like(out_grad)
+
+    def on_unit(unit):
+        columns = block_columns(unit)
+        got[:, columns] = dot(w_out[...], held[unit], 1, 1).astype(bf16)
+        out_grad[...] += dot(ot[:, columns], held[unit], 1, 0)
+
+    group_gather(length, grad, held, send, receive, on_unit)
+
+
+def spread(length, grad, w_out, ot):
+    rows, width = grad.shape
+    return remote_call(
+        functools.partial(spread_kernel, length), "spread", 3,
+        (like(ot.shape, bf16), like(w_out.shape, f32)), (IN_VMEM,) * 2, [IN_VMEM] * 3,
+        gather_scratch(2 * length, rows, width), grad, w_out, ot,
+    )
+
+
+def token_kernel(length, grads, joint, token_grad, *scratch):
+    greet(group_neighbours(length))
+    token_grad[...] = group_scatter(
+        length, lambda unit, half: dot(grads[:, half_columns(unit, half)], joint[...], 0, 0), *scratch
+    )
+
+
+def token_sum(length, grads, joint, rows):
+    width = joint.shape[1]
+    return remote_call(
+        functools.partial(token_kernel, length), "token_sum", 4,
+        like((rows, width), f32), IN_VMEM, [IN_VMEM] * 2, scatter_scratch(length, rows, width), grads, joint,
+    )
+
+
 def shards(
     tokens, lengths, w_query, w_key, w_value, s_qk, w_out, up_weight, gate_weight, down_weight,
     s_up, s_gate, alpha_attn, alpha_mlp, cotangent,
 ):
     units = up_weight.shape[0]
-    mlp_weight = gather(jnp.stack([up_weight, gate_weight, down_weight])[None], OWNERS)
     mlp_scale = gather(jnp.stack([s_up, s_gate])[None], OWNERS).astype(f32)
-    owners = mlp_weight.shape[0]
-    up_full, gate_full, down_full = (
-        mlp_weight[:, i].reshape(owners * units, -1) for i in range(3)
-    )
+    owners = mlp_scale.shape[0]
+    down_full = gather(down_weight, OWNERS)
     up_scale, gate_scale = (mlp_scale[:, i].reshape(1, owners * units) for i in range(2))
 
-    group_tokens = gather(tokens, GROUP)
-    rows = group_tokens.shape[0]
+    length = lax.axis_size("z")
+    own_rows, width = tokens.shape
+    rows = 4 * length * own_rows
     cosine, sine = turn_table(lengths[0], rows)
-    joint = jnp.concatenate([w_query, w_key, w_value], axis=1)
-    projected = dot(joint, group_tokens, 0, 1)
-    gain = s_qk[:, None]
-    turned_q = turn(projected[:HEAD_DIM], cosine, sine)
-    turned_k = turn(projected[HEAD_DIM : 2 * HEAD_DIM], cosine, sine)
-    qt = (unit_features(turned_q)[0] * gain).astype(bf16)
-    kt = (unit_features(turned_k)[0] * gain).astype(bf16)
-    vt = projected[2 * HEAD_DIM :].astype(bf16)
+    joint = jnp.concatenate([w_query, w_key, w_value], axis=1).T
+    group_tokens, turned_q, turned_k, qt, kt, vt = project(
+        length, tokens, joint, s_qk[:, None], cosine, sine
+    )
+    up_gate = jnp.stack([up_weight, gate_weight])[None]
+    qt, up_gate = lax.optimization_barrier((qt, up_gate))
+    up_gate = gather(up_gate, OWNERS)
+    up_full, gate_full = (up_gate[:, i].reshape(owners * units, -1) for i in range(2))
     ot, lse = attention_forward(lengths, qt, kt, vt)
-    branch = scatter_sum(dot(ot, w_out, 0, 0).astype(bf16), GROUP).astype(f32)
+    branch = branch_sum(length, ot, w_out, own_rows)
 
     hidden, front_pull = jax.vjp(front, branch, tokens.astype(f32), alpha_attn)
     hidden_low = gather(hidden.astype(bf16), PLANE)
@@ -233,16 +549,13 @@
     scale_grads = scatter_sum(scale_grads, OWNERS)[0]
     branch_grad, token_grad, alpha_attn_grad = front_pull(hidden_grad)
 
-    group_branch = gather(branch_grad.astype(bf16), GROUP)
-    got = dot(w_out, group_branch, 1, 1).astype(bf16)
-    out_grad = dot(ot, group_branch, 1, 0)
+    got, out_grad = spread(length, branch_grad.astype(bf16), w_out, ot)
     gqt, gkt, gvt = attention_backward(lengths, qt, kt, vt, ot, got, lse)
     gqt, query_gain_grad = features_back(turned_q, s_qk, gqt * (1.0 / ROOT), cosine, sine)
     gkt, key_gain_grad = features_back(turned_k, s_qk, gkt * (1.0 / ROOT), cosine, sine)
     joint_grad = jnp.concatenate([gqt, gkt, gvt], axis=0).astype(bf16)
-    token_part = dot(joint_grad, joint, 0, 1)
-    token_attn_grad = scatter_sum(token_part.astype(bf16), GROUP).astype(f32)
-    joint_weight_grad = dot(group_tokens, joint_grad, 0, 1)
+    token_attn_grad = token_sum(length, joint_grad, joint, own_rows)
+    joint_weight_grad = dot(group_tokens.reshape(rows, width), joint_grad, 0, 1)
     dp = ("o", "x")
     joint_weight_grad = lax.psum(joint_weight_grad.astype(bf16), dp).astype(f32)
     out_grad = lax.psum(out_grad.astype(bf16), dp).astype(f32)

time: 786 us -> 698 us (0.89)
  waiting for transfers between devices: 538 us -> 217 us
  Pallas kernels: 26 us -> 278 us
  matrix products: 74.8 us -> 51.6 us
    pallas_call x0 -> x4, Pallas kernels: none -> 252 us  [remote_call(): pl.pallas_call(kernel, name=name, out_shape=outs, in_specs=in_specs, out_...]
    all_gather x5 -> x4, waiting for transfers between devices: 238 us -> 77.1 us  [gather(): return lax.all_gather(values, axes, axis=0, tiled=True)]
    reduce_scatter x5 -> x3, waiting for transfers between devices: 299 us -> 139 us  [scatter_sum(): return lax.psum_scatter(values, axes, scatter_dimension=0, tiled=True)]
    dot_general x15 -> x10, matrix products: 74.8 us -> 51.6 us  [dot(): lax.dot_general(left, right, (((left_dim,), (right_dim,)), ((), ())), pre...]
  transfers between devices with their start and end apart: 11 -> 8, of which waited for: 8 -> 6; matrix products, arithmetic and copies ran while one was open for 9% -> 5% of each run, Pallas kernels for 2% -> 20%
where the time goes in v2:
time: 698 us; the launch traced here: 689 us
  Pallas kernels  278 us (40%)
  waiting for transfers between devices  217 us (31%)
  blocking collectives  68.7 us (10%)
  matrix products  51.6 us (7%)
  other arithmetic  44.8 us (6%)
  between operations  15.2 us (2%)
  local copies, waits for them, and re-layouts  13 us (2%)
    pallas_call x4, Pallas kernels, remote_call(): pl.pallas_call(kernel, name=name, out_shape=outs, in_specs=in_specs, out_...  252 us
    reduce_scatter x3, waiting for transfers between devices, scatter_sum(): return lax.psum_scatter(values, axes, scatter_dimension=0, tiled=True)  139 us
    all_gather x4, waiting for transfers between devices, gather(): return lax.all_gather(values, axes, axis=0, tiled=True)  77.1 us
    dot_general x10, matrix products, dot(): lax.dot_general(left, right, (((left_dim,), (right_dim,)), ((), ())), pre...  51.6 us
    psum x1, blocking collectives, shards(): alpha_sums = lax.psum(jnp.stack([alpha_attn_grad, alpha_mlp_grad]), AXES)  39.6 us
    pallas_call x2, Pallas kernels, attention_call(): pl.pallas_call(kernel, name=name, out_shape=outs, in_specs=[pl.BlockSpec(...  25.9 us
  transfers between devices with their start and end apart: 8, of which 6 were waited for; matrix products, arithmetic and copies ran while one was open for 5% of the time, Pallas kernels for 20%

profile of v2, /device:TPU:0, one launch (start us, length us, event | category | flops | bytes accessed | tf_op | source)
XLA Modules:
  0.0 689.1 jit_solution(4159234208962810105)
XLA Ops:
  9.5 1.9 maximum_bitcast_fusion
  11.4 2.8 multiply_sine_fusion
  14.2 1.8 maximum_bitcast_fusion.1.joint
  16.0 62.7 %project.1 = (bf16[8,512,1024]{2,1,0:T(8,128)(2,1)}, f32[64,4096]{1,0:T(8,128)}, f32[64,4096]{1,0:T(8,128)}, bf16[64,4096]{1,0:T(8,128)(2,1)}, bf16[64,4096]{1,0:T(8,128)(2,1)}, /*index=5*/bf16[64,4096]{1,0:T(8,128)(2,1)}) custom-call(bf16[256,1024]{1,0:T(8,128)(2,1)} %tokens.1, bf16[192,1024]{1,0:T(8,128)(2,1)} %maximum_bitcast_fusion.1.joint, ...), custom_call_target="tpu_custom_call" | custom-call | tf_op jit(solution)/shard_map/project/pallas_call | solution.py:383
  78.8 9.4 %attn_forward.1 = (bf16[64,4096]{1,0:T(8,128)(2,1)}, f32[1,4096]{1,0:T(1,128)}) custom-call(s32[1,4]{1,0:T(1,128)} %lengths.3, bf16[64,4096]{1,0:T(8,128)(2,1)} %get-tuple-element.30.qt, bf16[64,4096]{1,0:T(8,128)(2,1)} %get-tuple-element.31.kt, bf16[64,4096]{1,0:T(8,128)(2,1)} %get-tuple-element.32.vt), custom_call_target="tpu_custom_call" | custom-call | tf_op jit(solution)/shard_map/attn_forward/pallas_call | solution.py:109
  88.2 72.6 %branch_sum.1 = f32[256,1024]{1,0:T(8,128)} custom-call(bf16[64,4096]{1,0:T(8,128)(2,1)} %get-tuple-element.33.ot, bf16[64,1024]{1,0:T(8,128)(2,1)} %w_out.3), custom_call_target="tpu_custom_call" | custom-call | tf_op jit(solution)/shard_map/branch_sum/pallas_call | solution.py:383
  160.8 1.4 multiply_reduce_fusion.14
  162.2 1.7 multiply_reduce_fusion.13
  165.7 11.6 %all-gather.1 = bf16[4,2,128]{2,1,0:T(2,128)(2,1)S(1)} all-gather(bf16[1,2,128]{2,1,0:T(2,128)(2,1)S(1)} %maximum_bitcast_fusion.2), channel_id=2, replica_groups=mesh['o'=1,'x'=2,'z'=4,'y'=2,'c'=2] {'o','z'}, dimensions={0}, use_global_device_ids=true | all-gather | bytes 2560 | tf_op jit(solution)/shard_map/all_gather | solution.py:174
  177.3 1.8 fusion.33
  179.2 23.4 %all-gather.7.cloned.1.call-done = bf16[2048,1024]{1,0:T(8,128)(2,1)} async-done(((bf16[256,1024]{1,0:T(8,128)(2,1)}), bf16[2048,1024]{1,0:T(8,128)(2,1)}) %all-gather.7.cloned.1.call-update) | async-done | bytes 4194320 | tf_op jit(solution)/shard_map/all_gather | solution.py:174
  202.6 4.7 fusion.37
  207.3 1.9 copy-done.27
  209.3 5.9 multiply_convert_fusion.2
  215.1 17.0 %all-gather.11.cloned.1.call-done = bf16[512,1024]{1,0:T(8,128)(2,1)} async-done(((bf16[128,1024]{1,0:T(8,128)(2,1)}), bf16[512,1024]{1,0:T(8,128)(2,1)}) %all-gather.11.cloned.1.call-update) | async-done | bytes 1048592 | tf_op jit(solution)/shard_map/all_gather | solution.py:174
  232.1 6.2 convolution_convert_fusion
  238.4 50.9 %reduce-scatter.4.cloned.1.call-done = bf16[256,1024]{1,0:T(8,128)(2,1)} async-done(((bf16[2048,1024]{1,0:T(8,128)(2,1)}), bf16[256,1024]{1,0:T(8,128)(2,1)}) %reduce-scatter.4.cloned.1.call-update) | async-done | bytes 524304 | tf_op jit(solution)/shard_map/reduce_scatter | solution.py:178
  290.6 1.6 fusion.3
  292.3 2.4 fusion.8
  296.0 36.7 %all-gather.13.cloned.1.call-done = bf16[2048,1024]{1,0:T(8,128)(2,1)} async-done(((bf16[256,1024]{1,0:T(8,128)(2,1)}), bf16[2048,1024]{1,0:T(8,128)(2,1)}) %all-gather.13.cloned.1.call-update) | async-done | bytes 4194320 | tf_op jit(solution)/shard_map/all_gather | solution.py:174
  332.7 5.3 convolution_convert_fusion.1
  339.5 9.7 %multiply_reduce_fusion.1 = (f32[512]{0:T(512)S(1)}, f32[512]{0:T(512)S(1)}, f32[2048,512]{1,0:T(8,128)S(1)}, bf16[2048,512]{1,0:T(8,128)(2,1)S(1)}) fusion(f32[2048,512]{1,0:T(8,128)S(1)} %copy-done.29, f32[2048,512]{1,0:T(8,128)S(1)} %copy-done.28, f32[512]{0:T(512)S(1)} %bitcast.73, f32[512]{0:T(512)S(1)} %bitcast.79, ...), kind=kOutput, calls=%fused_computation.5 | convolution fusion | flops 2168454144 | bytes 19931136 | tf_op jit(solution)/shard_map/dot_general | solution.py:26
  349.2 2.4 convolution_convert_fusion.2
  351.9 2.3 convolution_convert_fusion.3
  354.3 2.0 pad_maximum_fusion
  356.6 4.3 fusion.38
  360.9 4.3 add_convert_fusion
  366.5 1.4 multiply_reduce_fusion.7
  368.0 12.1 %all-reduce = f32[4,2,128]{2,1,0:T(2,128)S(1)} all-reduce(f32[4,2,128]{2,1,0:T(2,128)S(1)} %pad_maximum_fusion.2), channel_id=6, replica_groups=mesh['o'=1,'x'=2,'z'=4,'y'=2,'c'=2] {'o','z'}, use_global_device_ids=true, to_apply=%region_24.25.clone | all-reduce | flops 1024 | bytes 8192
  381.2 35.7 %reduce-scatter.8.cloned.1.call-done = bf16[1,3,128,1024]{3,2,1,0:T(8,128)(2,1)} async-done(((bf16[4,3,128,1024]{3,2,1,0:T(8,128)(2,1)}), bf16[1,3,128,1024]{3,2,1,0:T(8,128)(2,1)}) %reduce-scatter.8.cloned.1.call-update) | async-done | bytes 786448 | tf_op jit(solution)/shard_map/reduce_scatter | solution.py:178
  419.4 52.7 %reduce-scatter.6.cloned.1.call-done = bf16[256,1024]{1,0:T(8,128)(2,1)} async-done(((bf16[2048,1024]{1,0:T(8,128)(2,1)}), bf16[256,1024]{1,0:T(8,128)(2,1)}) %reduce-scatter.6.cloned.1.call-update) | async-done | bytes 524304 | tf_op jit(solution)/shard_map/reduce_scatter | solution.py:178
  472.1 1.7 multiply_reduce_fusion.2
  473.8 1.9 multiply_reduce_fusion.3
  476.8 59.7 %spread.1 = (bf16[64,4096]{1,0:T(8,128)(2,1)}, f32[64,1024]{1,0:T(8,128)}) custom-call(bf16[256,1024]{1,0:T(8,128)(2,1)} %fusion.5.grad, bf16[64,1024]{1,0:T(8,128)(2,1)} %w_out.3, bf16[64,4096]{1,0:T(8,128)(2,1)} %get-tuple-element.33.ot), custom_call_target="tpu_custom_call" | custom-call | tf_op jit(solution)/shard_map/spread/pallas_call | solution.py:383
  536.6 1.6 convert_element_type.96
  538.2 16.4 %attn_backward.1 = (f32[64,4096]{1,0:T(8,128)}, f32[64,4096]{1,0:T(8,128)}, f32[64,4096]{1,0:T(8,128)}) custom-call(s32[1,4]{1,0:T(1,128)} %lengths.3, bf16[64,4096]{1,0:T(8,128)(2,1)} %get-tuple-element.30.qt, bf16[64,4096]{1,0:T(8,128)(2,1)} %get-tuple-element.31.kt, bf16[64,4096]{1,0:T(8,128)(2,1)} %get-tuple-element.32.vt, ...), custom_call_target="tpu_custom_call" | custom-call | tf_op jit(solution)/shard_map/attn_backward/pallas_call | solution.py:109
  554.6 2.3 multiply_reduce_fusion.4
  557.5 2.3 fusion.24
  559.8 2.3 fusion.23
  562.1 2.3 fusion.22
  564.3 2.3 fusion.21
  566.7 6.5 convolution_convert_fusion.4
  573.2 57.1 %token_sum.1 = f32[256,1024]{1,0:T(8,128)} custom-call(bf16[192,4096]{1,0:T(8,128)(2,1)} %copy-done.12, bf16[192,1024]{1,0:T(8,128)(2,1)} %maximum_bitcast_fusion.1.joint), custom_call_target="tpu_custom_call" | custom-call | tf_op jit(solution)/shard_map/token_sum/pallas_call | solution.py:383
  630.4 5.4 psum.29
  635.8 39.6 %psum.31 = f32[2,1024]{1,0:T(2,128)S(1)} all-reduce(f32[2,1024]{1,0:T(2,128)S(1)} %pad_maximum_fusion.1), channel_id=1, replica_groups=mesh['o'=1,'x'=2,'z'=4,'y'=2,'c'=2] {'o','x','z','y','c'}, use_global_device_ids=true, to_apply=%region_27.28 | all-reduce | flops 2048 | bytes 16384 | tf_op jit(solution)/shard_map/psum | solution.py:563
  676.0 2.2 add_convert_fusion.1
  678.3 1.6 convert_element_type.97
  679.9 1.9 fusion.34
  (112 shorter events, 16.1 us)
Async XLA Ops:
  7.2 170.1 %all-gather.9.cloned.1.call-start = ((), (), s32[]{:S(2)}) async-start(), calls=%async_computation.4 | async-start | bytes 2621440 | tf_op jit(solution)/shard_map/all_gather | solution.py:174
  11.4 150.8 %copy-start.7 = (bf16[256,1024]{1,0:T(8,128)(2,1)S(1)}, bf16[256,1024]{1,0:T(8,128)(2,1)}, u32[]{:S(2)}) copy-start(bf16[256,1024]{1,0:T(8,128)(2,1)} %tokens.1) | copy-start | bytes 1572868
  11.4 150.8 %copy-start.17 = (f32[1024]{0:T(1024)S(1)}, f32[1024]{0:T(1024)}, u32[]{:S(2)}) copy-start(f32[1024]{0:T(1024)} %param.27) | copy-start | bytes 12292
  78.8 123.8 %all-gather.7.cloned.1.call-start = ((), (), s32[]{:S(2)}) async-start(), calls=%async_computation.3 | async-start | bytes 4718592 | tf_op jit(solution)/shard_map/all_gather | solution.py:174
  88.2 77.4 %copy-start.23 = (bf16[128]{0:T(256)(128)(2,1)S(1)}, bf16[128]{0:T(256)(128)(2,1)}, u32[]{:S(2)}) copy-start(bf16[128]{0:T(256)(128)(2,1)} %param.26) | copy-start | bytes 772
  88.2 77.4 %copy-start.24 = (bf16[128]{0:T(256)(128)(2,1)S(1)}, bf16[128]{0:T(256)(128)(2,1)}, u32[]{:S(2)}) copy-start(bf16[128]{0:T(256)(128)(2,1)} %param.25) | copy-start | bytes 772
  164.8 67.3 %all-gather.11.cloned.1.call-start = ((), (), s32[]{:S(2)}) async-start(), calls=%async_computation.5 | async-start | bytes 1310720 | tf_op jit(solution)/shard_map/all_gather | solution.py:174
  165.6 123.7 %reduce-scatter.4.cloned.1.call-start = ((), (), s32[]{:S(2)}) async-start(), calls=%async_computation.6 | async-start | bytes 4718592 | tf_op jit(solution)/shard_map/reduce_scatter | solution.py:178
  179.1 28.2 %copy-start.15 = (bf16[4,1,128,1024]{3,2,1,0:T(8,128)(2,1)}, bf16[4,1,128,1024]{3,2,1,0:T(8,128)(2,1)S(1)}, u32[]{:S(2)}) copy-start(bf16[4,1,128,1024]{3,2,1,0:T(8,128)(2,1)S(1)} %get-tuple-element.67) | copy-start | bytes 3145732
  202.6 6.7 copy-start.19
  207.3 2.0 copy-start.27
  238.3 52.3 %copy-start.13 = (bf16[256,1024]{1,0:T(8,128)(2,1)S(1)}, bf16[256,1024]{1,0:T(8,128)(2,1)}, u32[]{:S(2)}) copy-start(bf16[256,1024]{1,0:T(8,128)(2,1)} %param.29) | copy-start | bytes 1572868
  238.3 52.3 %copy-start.16 = (f32[1024]{0:T(1024)S(1)}, f32[1024]{0:T(1024)}, u32[]{:S(2)}) copy-start(f32[1024]{0:T(1024)} %param.28) | copy-start | bytes 12292
  238.3 94.4 %all-gather.13.cloned.1.call-start = ((), (), s32[]{:S(2)}) async-start(), calls=%async_computation.7 | async-start | bytes 4718592 | tf_op jit(solution)/shard_map/all_gather | solution.py:174
  289.3 5.4 copy-start.1
  295.8 121.1 %reduce-scatter.8.cloned.1.call-start = ((), (), s32[]{:S(2)}) async-start(), calls=%async_computation.9 | async-start | bytes 3932160 | tf_op jit(solution)/shard_map/reduce_scatter | solution.py:178
  332.7 5.3 copy-start.21
  332.7 5.3 copy-start.22
  332.7 5.6 copy-start.28
  332.7 6.8 copy-start.29
  339.5 9.7 %copy-start.20 = (bf16[2048,1024]{1,0:T(8,128)(2,1)S(1)}, bf16[2048,1024]{1,0:T(8,128)(2,1)}, u32[]{:S(2)}) copy-start(bf16[2048,1024]{1,0:T(8,128)(2,1)} %all-gather.7.cloned.1.call-done) | copy-start | bytes 12582916
  349.2 2.4 copy-start.8
  349.2 2.7 copy-start.26
  356.3 115.8 %reduce-scatter.6.cloned.1.call-start = ((), (), s32[]{:S(2)}) async-start(), calls=%async_computation.8 | async-start | bytes 4718592 | tf_op jit(solution)/shard_map/reduce_scatter | solution.py:178
  356.6 4.4 copy-start.9
  365.3 0.7 copy-start.25
  365.3 1.2 copy-start.2
  365.3 2.7 copy-start.18
  365.3 312.9 %all-reduce.4.cloned.1.call-start = ((), (), s32[]{:S(2)}) async-start(), calls=%async_computation.10 | async-start | bytes 1048576 | tf_op jit(solution)/shard_map/psum | solution.py:560
  381.2 92.6 %copy-start = (f32[256,1024]{1,0:T(8,128)S(1)}, f32[256,1024]{1,0:T(8,128)}, u32[]{:S(2)}) copy-start(f32[256,1024]{1,0:T(8,128)} %branch_sum.1) | copy-start | bytes 3145732
  475.7 81.3 %copy-start.5 = (f32[256,1024]{1,0:T(8,128)}, f32[256,1024]{1,0:T(8,128)S(1)}, u32[]{:S(2)}) copy-start(f32[256,1024]{1,0:T(8,128)S(1)} %get-tuple-element.59) | copy-start | bytes 3145732
  475.7 78.9 %copy-start.3 = (f32[64,4096]{1,0:T(8,128)S(1)}, f32[64,4096]{1,0:T(8,128)}, u32[]{:S(2)}) copy-start(f32[64,4096]{1,0:T(8,128)} %get-tuple-element.35) | copy-start | bytes 3145732
  475.7 78.9 %copy-start.4 = (f32[64,4096]{1,0:T(8,128)S(1)}, f32[64,4096]{1,0:T(8,128)}, u32[]{:S(2)}) copy-start(f32[64,4096]{1,0:T(8,128)} %get-tuple-element.39) | copy-start | bytes 3145732
  554.6 2.4 copy-start.10
  554.6 2.4 copy-start.11
  557.5 9.1 %copy-start.14 = (f32[64,4096]{1,0:T(8,128)S(1)}, f32[64,4096]{1,0:T(8,128)}, u32[]{:S(2)}) copy-start(f32[64,4096]{1,0:T(8,128)} %get-tuple-element.41) | copy-start | bytes 3145732
  566.7 6.5 copy-start.12
  573.2 102.8 %copy-start.6 = (f32[256,1024]{1,0:T(8,128)S(1)}, f32[256,1024]{1,0:T(8,128)}, u32[]{:S(2)}) copy-start(f32[256,1024]{1,0:T(8,128)} %copy-done.5) | copy-start | bytes 3145732
Sparse Core Ops, SparseCore 0:
  78.9 58.2 all-gather.8
  165.0 37.5 all-gather.6
  204.2 27.9 all-gather.10
  238.4 50.8 reduce-scatter.3
  295.9 36.7 all-gather.12
  356.4 60.4 reduce-scatter.7
  420.6 51.4 reduce-scatter.5
  573.3 28.6 all-reduce.3

commit v3 on v2

--- a/solution.py
+++ b/solution.py
@@ -16,8 +16,6 @@
 SCORE_SCALE = math.log2(math.e) / ROOT
 AXES = ("o", "x", "z", "y", "c")
 GROUP = ("z", "y", "c")
-PLANE = ("x", "y", "c")
-OWNERS = ("o", "z")
 f32, bf16 = jnp.float32, jnp.bfloat16
 VMEM_LIMIT = 56 * 2**20
 
@@ -127,10 +125,6 @@
     return attention_call(attention_backward_kernel, "attn_backward", outs, lengths, *operands)
 
 
-def sphere(values):
-    return values * lax.rsqrt(jnp.mean(values * values, axis=-1, keepdims=True) + EPSILON)
-
-
 def turn_table(lengths_row, rows):
     ends = jnp.sum(jnp.where(jnp.tri(lengths_row.shape[0], dtype=bool), lengths_row[None, :], 0), 1)
     row = jnp.arange(rows, dtype=jnp.int32)
@@ -153,29 +147,8 @@
     return turned * scale, scale
 
 
-def features_back(turned, gain, grad, cosine, sine):
-    normal, scale = unit_features(turned)
-    gain_grad = jnp.sum(grad * normal, axis=1)
-    grad = grad * gain[:, None]
-    grad = scale * (grad - normal * jnp.mean(grad * normal, axis=0, keepdims=True))
-    return turn(grad, cosine, -sine), gain_grad
-
-
-def front(branch, own_tokens, alpha):
-    return sphere(own_tokens + alpha * (sphere(branch) - own_tokens))
-
-
-def core(up_proj, gate_proj, up_scale, gate_scale):
-    gated = gate_proj * gate_scale
-    return up_proj * up_scale * (gated * jax.nn.sigmoid(gated))
-
-
 def gather(values, axes):
     return lax.all_gather(values, axes, axis=0, tiled=True)
-
-
-def scatter_sum(values, axes):
-    return lax.psum_scatter(values, axes, scatter_dimension=0, tiled=True)
 
 
 MESH_ID = pl.DeviceIdType.MESH
@@ -227,7 +200,7 @@
     ]
 
 
-def group_gather(length, own, held, send, receive, on_unit):
+def group_gather(length, own, held, send, receive, on_unit, at_step=None):
     z, y, c = here("z", "y", "c")
     rows = held.shape[1] // 2
 
@@ -261,6 +234,8 @@
             if step > 0:
                 arrived(order[step], y, c)
             passed_on(order[step], lambda copy_: copy_.start())
+        if at_step is not None:
+            at_step(step)
         if step > 0:
             zz = order[step - 1]
             arrived(zz, y, 1 - c)
@@ -297,7 +272,7 @@
     ]
 
 
-def group_scatter(length, produce, own, cross, across, along, cross_sem, across_sem, along_sem, between=None):
+def group_scatter(length, produce, own, cross, across, along, cross_sem, across_sem, along_sem, prepare=None, between=None, at_step=None):
     z, y, c = here("z", "y", "c")
 
     def to_core(unit):
@@ -318,6 +293,8 @@
     def first(zz):
         for yy in (1 - y, y):
             unit = zz * 2 + yy
+            if prepare is not None:
+                prepare(unit)
             cross[0, unit] = produce(unit, 1 - c).astype(bf16)
             to_core(unit).start()
         for yy in (1 - y, y):
@@ -363,6 +340,8 @@
     for step in range(length + 2):
         if step < length:
             first(order[step])
+        if at_step is not None:
+            at_step(step)
         if 1 <= step <= length:
             second(order[step - 1])
         if step == length and between is not None:
@@ -401,6 +380,159 @@
     return jax.ShapeDtypeStruct(shape, dtype)
 
 
+class LineGather:
+    def __init__(self, length, own, held, send, receive, local_sem):
+        self.length, self.own, self.held = length, own, held
+        self.sems, self.local_sem = (send, receive), local_sem
+        self.z = lax.axis_index("z")
+
+    def copy(self, way, zz, source=None):
+        send, receive = self.sems
+        at = self.held.at[zz]
+        device = {"z": self.z + 1} if way == 0 else {"z": self.z - 1}
+        return remote(at if source is None else source, at, send.at[way, zz], receive.at[zz], device)
+
+    def ways(self, d, act):
+        z, length = self.z, self.length
+        for way, zz, there, more in (
+            (0, z - d, z - d >= 0, z < length - 1),
+            (1, z + d, z + d < length, z > 0),
+        ):
+            act(way, zz, there, there & more)
+
+    def stage(self, d):
+        z = self.z
+        if d == 0:
+            pltpu.make_async_copy(self.own, self.held.at[z], self.local_sem).start()
+
+        def begin(way, zz, there, more):
+            if d > 0:
+
+                @pl.when(there)
+                def _():
+                    self.arrival(way, zz).wait_recv()
+
+            if d < self.length - 1:
+
+                @pl.when(more)
+                def _():
+                    self.copy(way, zz, self.own if d == 0 else None).start()
+
+        if d < self.length:
+            self.ways(d, begin)
+            return
+        for e in range(self.length - 1):
+
+            def finish(way, zz, there, more):
+                @pl.when(more)
+                def _():
+                    self.copy(way, zz, self.own if e == 0 else None).wait_send()
+
+            self.ways(e, finish)
+        pltpu.make_async_copy(self.own, self.held.at[z], self.local_sem).wait()
+
+    def arrival(self, way, zz):
+        send, receive = self.sems
+        at = self.held.at[zz]
+        return remote(at, at, send.at[way, zz], receive.at[zz], {"c": 1 - lax.axis_index("c")})
+
+
+def line_gather_semaphores(length):
+    return [
+        pltpu.SemaphoreType.DMA((2, length)),
+        pltpu.SemaphoreType.DMA((length,)),
+        pltpu.SemaphoreType.DMA,
+    ]
+
+
+class LineScatter:
+    def __init__(self, length, parts, sums, moving, sems):
+        self.length, self.parts, self.sums, self.moving, self.sems = length, parts, sums, moving, sems
+        self.z = lax.axis_index("z")
+        self.count = parts.shape[1]
+        self.order = [line_order(self.z, length, length - 1 - step) for step in range(length)]
+        self.items = [(i, step) for step in range(length - 1) for i in range(self.count)]
+
+    def copy(self, i, zz, slot, device):
+        return remote(
+            self.moving.at[0, zz, i], self.moving.at[slot, zz, i],
+            self.sems.at[0, zz, i], self.sems.at[slot, zz, i], device,
+        )
+
+    def summed(self, i, zz, store):
+        z, length = self.z, self.length
+        aside = {"c": 1 - lax.axis_index("c")}
+        below, above = (zz >= z) & (z > 0), (zz <= z) & (z < length - 1)
+
+        def value(slots):
+            total = self.parts[zz, i].astype(f32)
+            for slot in slots:
+                total = total + self.moving[slot, zz, i].astype(f32)
+            return total
+
+        for slot, condition in ((1, below), (2, above)):
+
+            @pl.when(condition)
+            def _():
+                self.copy(i, zz, slot, aside).wait_recv()
+
+        @pl.when(below & above)
+        def _():
+            store(value((1, 2)))
+
+        @pl.when(below & jnp.logical_not(above))
+        def _():
+            store(value((1,)))
+
+        @pl.when(above & jnp.logical_not(below))
+        def _():
+            store(value((2,)))
+
+        @pl.when(jnp.logical_not(above | below))
+        def _():
+            store(value(()))
+
+    def item(self, i, step):
+        zz = self.order[step]
+
+        def store(total):
+            self.moving[0, zz, i] = total.astype(bf16)
+
+        self.summed(i, zz, store)
+
+        @pl.when(zz > self.z)
+        def _():
+            self.copy(i, zz, 1, {"z": self.z + 1}).start()
+
+        @pl.when(zz < self.z)
+        def _():
+            self.copy(i, zz, 2, {"z": self.z - 1}).start()
+
+    def hook(self, h, pace=2):
+        at_end = (self.z == 0) | (self.z == self.length - 1)
+        for late, condition in ((0, at_end), (1, jnp.logical_not(at_end))):
+            share = self.items[max(0, (h - late) * pace) : max(0, (h - late + 1) * pace)]
+            if share:
+
+                @pl.when(condition)
+                def _():
+                    for i, step in share:
+                        self.item(i, step)
+
+    def finish(self, hooks, pace=2):
+        while (hooks - 1) * pace < len(self.items):
+            self.hook(hooks, pace)
+            hooks += 1
+        for i in range(self.count):
+
+            def store(total):
+                self.sums[i] = total
+
+            self.summed(i, self.order[self.length - 1], store)
+        for i, step in self.items:
+            self.copy(i, self.order[step], 1, {"c": 1 - lax.axis_index("c")}).wait_send()
+
+
 def project_kernel(
     length, tokens, joint, gain, cosine, sine, gathered, turned_q, turned_k, qt, kt, vt,
     held, send, receive, out_sem,
@@ -444,54 +576,489 @@
     return pl.ds(pl.multiple_of(unit * BLOCK + half * rows, rows), rows)
 
 
-def branch_kernel(length, ot, w_out, branch, *scratch):
+def branch_kernel(length, ot, w_out, weight, branch, weights, send, receive, local_sem, *scratch):
     greet(group_neighbours(length))
+    line = LineGather(length, weight, weights, send, receive, local_sem)
+    stages = {0: 0, 3: 1, 5: 2}
+
+    def at_step(step):
+        if step in stages:
+            line.stage(stages[step])
+
     branch[...] = group_scatter(
-        length, lambda unit, half: dot(ot[:, half_columns(unit, half)], w_out[...], 0, 0), *scratch
-    )
-
-
-def branch_sum(length, ot, w_out, rows):
+        length, lambda unit, half: dot(ot[:, half_columns(unit, half)], w_out[...], 0, 0), *scratch,
+        at_step=at_step,
+    )
+    for stage in range(1, length + 1):
+        if stage not in stages.values():
+            line.stage(stage)
+
+
+def branch_sum(length, ot, w_out, weight, rows):
     width = w_out.shape[1]
     return remote_call(
         functools.partial(branch_kernel, length), "branch_sum", 2,
-        like((rows, width), f32), IN_VMEM, [IN_VMEM] * 2, scatter_scratch(length, rows, width), ot, w_out,
-    )
-
-
-def spread_kernel(length, grad, w_out, ot, got, out_grad, held, send, receive):
+        (like((rows, width), f32), like((length, *weight.shape), bf16)), (IN_VMEM, ANYWHERE),
+        [IN_VMEM] * 2 + [ANYWHERE], line_gather_semaphores(length) + scatter_scratch(length, rows, width),
+        ot, w_out, weight,
+    )
+
+
+def spread_kernel(
+    length, grad, w_out, ot, parts, got, out_grad, sums, held, send, receive, moving, moving_sem
+):
     greet(group_neighbours(length))
     out_grad[...] = jnp.zeros_like(out_grad)
+    line = LineScatter(length, parts, sums, moving, moving_sem)
 
     def on_unit(unit):
         columns = block_columns(unit)
         got[:, columns] = dot(w_out[...], held[unit], 1, 1).astype(bf16)
         out_grad[...] += dot(ot[:, columns], held[unit], 1, 0)
 
-    group_gather(length, grad, held, send, receive, on_unit)
-
-
-def spread(length, grad, w_out, ot):
+    group_gather(length, grad, held, send, receive, on_unit, line.hook)
+    line.finish(length + 1)
+
+
+def spread(length, grad, w_out, ot, parts):
     rows, width = grad.shape
+    _, count, units, _ = parts.shape
     return remote_call(
         functools.partial(spread_kernel, length), "spread", 3,
-        (like(ot.shape, bf16), like(w_out.shape, f32)), (IN_VMEM,) * 2, [IN_VMEM] * 3,
-        gather_scratch(2 * length, rows, width), grad, w_out, ot,
-    )
-
-
-def token_kernel(length, grads, joint, token_grad, *scratch):
-    greet(group_neighbours(length))
-    token_grad[...] = group_scatter(
-        length, lambda unit, half: dot(grads[:, half_columns(unit, half)], joint[...], 0, 0), *scratch
-    )
-
-
-def token_sum(length, grads, joint, rows):
-    width = joint.shape[1]
+        (like(ot.shape, bf16), like(w_out.shape, f32), like((count, units, width), f32)), (IN_VMEM,) * 3,
+        [IN_VMEM] * 4,
+        gather_scratch(2 * length, rows, width)
+        + [pltpu.VMEM((3, *parts.shape), bf16), pltpu.SemaphoreType.DMA((3, length, count))],
+        grad, w_out, ot, parts,
+    )
+
+
+def flip(position, bit):
+    return position + bit - 2 * bit * ((position // bit) % 2)
+
+
+def inward_kernel(
+    length, gqt, gkt, gvt, turned_q, turned_k, gain, cosine, sine, joint, gathered, out_grad, alpha_grads,
+    scale_grads, direct, token_grad, weight_grads, alpha_sums, scale_sums, gain_grad,
+    grads, held, held_sem, gains, gain_sem, sent, taken, weight_sem, small_out, small_in, small_sem,
+    *scratch,
+):
+    x, z, y, c = here("x", "z", "y", "c")
+    to_x = {"x": 1 - x}
+    bits = [1 << i for i in range(length.bit_length() - 1)]
+    greet(group_neighbours(length) + [(x >= 0, to_x)] + [(x >= 0, {"z": flip(z, bit)}) for bit in bits])
+    partners = [{"c": 1 - c}, {"y": 1 - y}, to_x] + [{"z": flip(z, bit)} for bit in bits]
+    load = pltpu.make_async_copy(gathered, held, held_sem)
+    load.start()
+    gains[0] = jnp.zeros_like(gains[0])
+    small_out[0] = jnp.zeros_like(small_out[0])
+    small_out[0, 0:2] = alpha_grads[...]
+    small_out[0, 2:4, : scale_grads.shape[1]] = scale_grads[...]
+
+    def exchange(i):
+        return remote(small_out.at[i], small_in.at[i], small_sem.at[0, i], small_sem.at[1, i], partners[i])
+
+    def at_step(step):
+        if 0 < step <= len(partners):
+            exchange(step - 1).wait_recv()
+            small_out[step] = small_out[step - 1]
+            summed = 2 if step <= 3 else 4
+            small_out[step, :summed] += small_in[step - 1, :summed]
+        if step < len(partners):
+            exchange(step).start()
+
+    def prepare(unit):
+        columns = block_columns(unit)
+        for part, turned, outer in ((0, turned_q, gqt), (1, turned_k, gkt)):
+            normal, scale = unit_features(turned[:, columns])
+            grad = outer[:, columns] * (1.0 / ROOT)
+            product = grad * normal
+            width = gains.shape[2]
+            for i in range(BLOCK // width):
+                gains[0] += product[:, i * width : (i + 1) * width]
+            grad = grad * gain[...]
+            grad = scale * (grad - normal * jnp.mean(grad * normal, axis=0, keepdims=True))
+            grad = turn(grad, cosine[:, columns], -sine[:, columns])
+            grads[part * HEAD_DIM : (part + 1) * HEAD_DIM, columns] = grad.astype(bf16)
+        grads[2 * HEAD_DIM :, columns] = gvt[:, columns].astype(bf16)
+
+    gain_copy = remote(gains.at[0], gains.at[1], gain_sem.at[0], gain_sem.at[1], to_x)
+    weight_copy = remote(sent, taken, weight_sem.at[0], weight_sem.at[1], to_x)
+
+    def between():
+        gain_copy.start()
+        load.wait()
+        rows = grads.shape[1]
+        product = dot(grads[...], held[...].reshape(rows, held.shape[2]), 1, 0)
+        sent[: 3 * HEAD_DIM] = product.astype(bf16)
+        sent[3 * HEAD_DIM :] = out_grad[...].astype(bf16)
+        weight_copy.start()
+
+    total = group_scatter(
+        length, lambda unit, half: dot(grads[:, half_columns(unit, half)], joint[...], 0, 0), *scratch,
+        prepare=prepare, between=between, at_step=at_step,
+    )
+    token_grad[...] = (direct[...] + total).astype(bf16)
+    for step in range(length + 2, len(partners) + 1):
+        at_step(step)
+    alpha_sums[...] = small_out[len(partners), 0:2]
+    scale_sums[...] = small_out[len(partners), 2:4, : scale_sums.shape[1]]
+    gain_copy.wait()
+    gain_grad[...] = jnp.sum(gains[0] + gains[1], axis=1, keepdims=True)
+    weight_copy.wait()
+    weight_grads[...] = sent[...].astype(f32) + taken[...].astype(f32)
+    for i in range(len(partners)):
+        exchange(i).wait_send()
+
+
+def inward(length, gathered, direct, out_grad, alpha_grads, scale_grads, *operands):
+    rows, width = direct.shape
+    units, block, _ = gathered.shape
+    exchanges = 3 + length.bit_length() - 1
+    small = (exchanges + 1, 4, width)
+    weights = (4 * HEAD_DIM, width)
+    scratch = [
+        pltpu.VMEM((3 * HEAD_DIM, units * block), bf16),
+        pltpu.VMEM(gathered.shape, bf16),
+        pltpu.SemaphoreType.DMA,
+        pltpu.VMEM((2, HEAD_DIM, 128), f32),
+        pltpu.SemaphoreType.DMA((2,)),
+        pltpu.VMEM(weights, bf16),
+        pltpu.VMEM(weights, bf16),
+        pltpu.SemaphoreType.DMA((2,)),
+        pltpu.VMEM(small, f32),
+        pltpu.VMEM(small, f32),
+        pltpu.SemaphoreType.DMA((2, exchanges)),
+    ]
     return remote_call(
-        functools.partial(token_kernel, length), "token_sum", 4,
-        like((rows, width), f32), IN_VMEM, [IN_VMEM] * 2, scatter_scratch(length, rows, width), grads, joint,
+        functools.partial(inward_kernel, length), "inward", 4,
+        (
+            like((rows, width), bf16), like(weights, f32), like(alpha_grads.shape, f32),
+            like(scale_grads.shape, f32), like((HEAD_DIM, 1), f32),
+        ),
+        (IN_VMEM,) * 5, [IN_VMEM] * 9 + [ANYWHERE] + [IN_VMEM] * 4,
+        scratch + scatter_scratch(length, rows, width),
+        *operands, gathered, out_grad, alpha_grads, scale_grads, direct,
+    )
+
+
+def plane_neighbours():
+    x, y, c = here("x", "y", "c")
+    return [(x >= 0, {"x": 1 - x}), (x >= 0, {"y": 1 - y}), (x >= 0, {"c": 1 - c})]
+
+
+def plane_gather(held, send, receive, on_pair):
+    x, y, c = here("x", "y", "c")
+    rows = held.shape[1] // 2
+    half = rows // 2
+    q0, qx, qy, qd = x * 2 + y, (1 - x) * 2 + y, x * 2 + 1 - y, (1 - x) * 2 + 1 - y
+    to_x, to_y, to_c = (0, {"x": 1 - x}), (1, {"y": 1 - y}), (2, {"c": 1 - c})
+
+    def copy(way, q, cc, h):
+        at = held.at[q, pl.ds(pl.multiple_of(cc * rows + h * half, half), half)]
+        return remote(at, at, send.at[way[0], q * 2 + h], receive.at[(q * 2 + cc) * 2 + h], way[1])
+
+    def arrived(q, cc, h):
+        copy(to_c, q, cc, h).wait_recv()
+
+    sent = []
+
+    def start(way, q, h):
+        sent.append((way, q, h))
+        copy(way, q, c, h).start()
+
+    start(to_x, q0, 0)
+    start(to_y, q0, 1)
+    start(to_c, q0, 0)
+    start(to_c, q0, 1)
+    start(to_x, q0, 1)
+    start(to_y, q0, 0)
+    for h in (0, 1):
+        arrived(q0, 1 - c, h)
+    on_pair(q0)
+    arrived(qx, c, 0)
+    start(to_y, qx, 0)
+    start(to_c, qx, 0)
+    arrived(qy, c, 1)
+    start(to_x, qy, 1)
+    start(to_c, qy, 1)
+    arrived(qx, c, 1)
+    start(to_c, qx, 1)
+    arrived(qy, c, 0)
+    start(to_c, qy, 0)
+    for q in (qx, qy):
+        for h in (0, 1):
+            arrived(q, 1 - c, h)
+        on_pair(q)
+    for h in (0, 1):
+        arrived(qd, c, h)
+        start(to_c, qd, h)
+    for h in (0, 1):
+        arrived(qd, 1 - c, h)
+    on_pair(qd)
+    for way, q, h in sent:
+        copy(way, q, c, h).wait_send()
+
+
+def plane_scatter(produce, own, cross, side, cross_sem, side_sem, between=None):
+    x, y, c = here("x", "y", "c")
+    rows = own.shape[1]
+    half = rows // 2
+    q0, qx, qy, qd = x * 2 + y, (1 - x) * 2 + y, x * 2 + 1 - y, (1 - x) * 2 + 1 - y
+    to_x, to_y = {"x": 1 - x}, {"y": 1 - y}
+
+    def to_core(q):
+        return remote(cross.at[0, q], cross.at[1, q], cross_sem.at[0, q], cross_sem.at[1, q], {"c": 1 - c})
+
+    def beside(kind, h, device):
+        part = pl.ds(h * half, half)
+        return remote(
+            side.at[0, kind, part], side.at[1, kind, part], side_sem.at[0, kind, h], side_sem.at[1, kind, h], device
+        )
+
+    def first(q):
+        cross[0, q] = produce(q, 1 - c).astype(bf16)
+        to_core(q).start()
+        own[q] = produce(q, c)
+
+    def joined(q):
+        to_core(q).wait_recv()
+        own[q] += cross[1, q].astype(f32)
+
+    def send(kind, q, h, device):
+        part = pl.ds(h * half, half)
+        side[0, kind, part] = own[q, part].astype(bf16)
+        beside(kind, h, device).start()
+
+    def add(q, kind, h, device):
+        part = pl.ds(h * half, half)
+        beside(kind, h, device).wait_recv()
+        own[q, part] += side[1, kind, part].astype(f32)
+
+    first(qd)
+    first(qx)
+    joined(qd)
+    send(0, qd, 0, to_x)
+    send(0, qd, 1, to_y)
+    first(qy)
+    joined(qx)
+    send(1, qx, 0, to_x)
+    joined(qy)
+    send(2, qy, 1, to_y)
+    first(q0)
+    add(qx, 0, 1, to_y)
+    send(1, qx, 1, to_x)
+    add(qy, 0, 0, to_x)
+    send(2, qy, 0, to_y)
+    joined(q0)
+    if between is not None:
+        between()
+    for h in (0, 1):
+        add(q0, 1, h, to_x)
+        add(q0, 2, 1 - h, to_y)
+    for q in (q0, qx, qy, qd):
+        to_core(q).wait_send()
+    beside(0, 0, to_x).wait_send()
+    beside(0, 1, to_y).wait_send()
+    for h in (0, 1):
+        beside(1, h, to_x).wait_send()
+        beside(2, h, to_y).wait_send()
+
+
+def mean_of(values):
+    return jnp.mean(values, axis=-1, keepdims=True)
+
+
+def scale_of(values):
+    return lax.rsqrt(mean_of(values * values) + EPSILON)
+
+
+def step_forward(target, start, alpha):
+    target_scale = scale_of(target)
+    unit = target * target_scale
+    moved = start + alpha * (unit - start)
+    moved_scale = scale_of(moved)
+    return moved * moved_scale, unit, target_scale, moved_scale
+
+
+def step_back(grad, result, unit, target_scale, moved_scale, start, alpha):
+    moved_grad = moved_scale * (grad - result * mean_of(grad * result))
+    unit_grad = alpha * moved_grad
+    target_grad = target_scale * (unit_grad - unit * mean_of(unit_grad * unit))
+    return target_grad, moved_grad - unit_grad, moved_grad * (unit - start)
+
+
+CHUNK = 32
+SCALE_ROWS = 16
+
+
+def mlp_kernel(
+    length, branch, tokens, alpha_attn, alpha_mlp, cotangent, up_gate, own_down, up_scale, gate_scale,
+    mixed, branch_low, token_grad, alpha_grads, weight_grads, scale_grads,
+    hidden, hidden_grad, held, grads, ups, gates, inner, up_low, gate_low, own, cross, side,
+    gather_send, gather_receive, cross_sem, side_sem, down, down_send, down_receive, down_local,
+):
+    x, z, y, c = here("x", "z", "y", "c")
+    rows, width = branch.shape
+    owners, units = length, own_down.shape[0]
+    full = owners * units
+    q0 = x * 2 + y
+    greet(plane_neighbours() + [(z > 0, {"z": z - 1}), (z < length - 1, {"z": z + 1})])
+    line = LineGather(length, own_down, down, down_send, down_receive, down_local)
+    line.stage(0)
+    done = []
+
+    def each_chunk(body):
+        def step(i, carry):
+            start = pl.multiple_of(i * CHUNK, CHUNK)
+            body(pl.ds(start, CHUNK), pl.ds(pl.multiple_of(c * rows + start, CHUNK), CHUNK))
+            return carry
+
+        lax.fori_loop(0, rows // CHUNK, step, 0)
+
+    def each_half(body):
+        def step(i, carry):
+            body(pl.ds(pl.multiple_of(i * rows, rows), rows))
+            return carry
+
+        lax.fori_loop(0, 2, step, 0)
+
+    def weight(i):
+        return up_gate[:, i, :units].reshape(full, width)
+
+    def down_weight():
+        return down[...].reshape(full, width)
+
+    def half_rows(half):
+        return pl.ds(pl.multiple_of(half * rows, rows), rows)
+
+    alpha_grads[...] = jnp.zeros_like(alpha_grads)
+    scale_grads[...] = jnp.zeros_like(scale_grads)
+
+    def enter(part, place):
+        result = step_forward(branch[part], tokens[part].astype(f32), alpha_attn[...])[0]
+        hidden[part] = result
+        held[q0, place] = result.astype(bf16)
+
+    each_chunk(enter)
+
+    def forward(q):
+        def half(part):
+            block = held[q, part]
+            up = dot(block, weight(0), 1, 1)
+            gate = dot(block, weight(1), 1, 1)
+            ups[q, part] = up
+            gates[q, part] = gate
+            gated = gate * gate_scale[...]
+            inner[q, part] = (up * up_scale[...] * (gated * jax.nn.sigmoid(gated))).astype(bf16)
+
+        each_half(half)
+        done.append(q)
+        if len(done) in stages:
+            line.stage(stages[len(done)])
+
+    stages = {1: 1, 3: 2}
+    plane_gather(held, gather_send.at[0], gather_receive.at[0], forward)
+    for stage in range(3, length + 1):
+        line.stage(stage)
+    plane_scatter(
+        lambda q, half: dot(inner[q, half_rows(half)], down_weight(), 1, 0),
+        own, cross, side, cross_sem.at[0], side_sem.at[0],
+    )
+
+    def turn_back(part, place):
+        start, alpha = hidden[part], alpha_mlp[...]
+        result, unit, target_scale, moved_scale = step_forward(own[q0, part], start, alpha)
+        mixed[part] = result.astype(bf16)
+        target_grad, start_grad, alpha_part = step_back(
+            cotangent[part].astype(f32), result, unit, target_scale, moved_scale, start, alpha
+        )
+        alpha_grads[1:2] += jnp.sum(alpha_part, axis=0, keepdims=True)
+        hidden_grad[part] = start_grad
+        grads[q0, place] = target_grad.astype(bf16)
+
+    each_chunk(turn_back)
+
+    def backward(q):
+        def half(part):
+            inner_grad = dot(grads[q, part], down_weight(), 1, 1)
+            up, gate = ups[q, part], gates[q, part]
+            gated = gate * gate_scale[...]
+            share = jax.nn.sigmoid(gated)
+            silu = gated * share
+            lifted = inner_grad * up
+            gated_grad = lifted * up_scale[...] * (share * (1.0 + gated * (1.0 - share)))
+            up_low[q, part] = (inner_grad * up_scale[...] * silu).astype(bf16)
+            gate_low[q, part] = (gated_grad * gate_scale[...]).astype(bf16)
+            scale_grads[0:1] += jnp.sum(lifted * silu, axis=0, keepdims=True)
+            scale_grads[1:2] += jnp.sum(gated_grad * gate, axis=0, keepdims=True)
+
+        each_half(half)
+
+    plane_gather(grads, gather_send.at[1], gather_receive.at[1], backward)
+
+    def weights_back():
+        tall = 4 * 2 * rows
+        for i, (left, right) in enumerate(((up_low, held), (gate_low, held), (inner, grads))):
+
+            def step(n, carry):
+                columns = pl.ds(pl.multiple_of(n * BLOCK, BLOCK), BLOCK)
+                product = dot(
+                    left[...].reshape(tall, full), right[:, :, columns].reshape(tall, BLOCK), 0, 0
+                )
+                weight_grads[:, i, :, columns] = product.astype(bf16).reshape(owners, units, BLOCK)
+                return carry
+
+            lax.fori_loop(0, width // BLOCK, step, 0)
+
+    plane_scatter(
+        lambda q, half: dot(up_low[q, half_rows(half)], weight(0), 1, 0)
+        + dot(gate_low[q, half_rows(half)], weight(1), 1, 0),
+        own, cross, side, cross_sem.at[1], side_sem.at[1], weights_back,
+    )
+
+    def leave(part, place):
+        start, alpha = tokens[part].astype(f32), alpha_attn[...]
+        result, unit, target_scale, moved_scale = step_forward(branch[part], start, alpha)
+        target_grad, start_grad, alpha_part = step_back(
+            hidden_grad[part] + own[q0, part], result, unit, target_scale, moved_scale, start, alpha
+        )
+        alpha_grads[0:1] += jnp.sum(alpha_part, axis=0, keepdims=True)
+        branch_low[part] = target_grad.astype(bf16)
+        token_grad[part] = start_grad
+
+    each_chunk(leave)
+
+
+def mlp(length, branch, tokens, alpha_attn, alpha_mlp, cotangent, up_gate, down, up_scale, gate_scale):
+    rows, width = branch.shape
+    owners, units = length, down.shape[0]
+    full = owners * units
+    low, wide = like((rows, width), bf16), like((rows, width), f32)
+    scratch = [
+        pltpu.VMEM((rows, width), f32),
+        pltpu.VMEM((rows, width), f32),
+        pltpu.VMEM((4, 2 * rows, width), bf16),
+        pltpu.VMEM((4, 2 * rows, width), bf16),
+        pltpu.VMEM((4, 2 * rows, full), f32),
+        pltpu.VMEM((4, 2 * rows, full), f32),
+        pltpu.VMEM((4, 2 * rows, full), bf16),
+        pltpu.VMEM((4, 2 * rows, full), bf16),
+        pltpu.VMEM((4, 2 * rows, full), bf16),
+        pltpu.VMEM((4, rows, width), f32),
+        pltpu.VMEM((2, 4, rows, width), bf16),
+        pltpu.VMEM((2, 3, rows, width), bf16),
+        pltpu.SemaphoreType.DMA((2, 3, 8)),
+        pltpu.SemaphoreType.DMA((2, 16)),
+        pltpu.SemaphoreType.DMA((2, 2, 4)),
+        pltpu.SemaphoreType.DMA((2, 2, 3, 2)),
+        pltpu.VMEM((length, *down.shape), bf16),
+    ] + line_gather_semaphores(length)
+    return remote_call(
+        functools.partial(mlp_kernel, length), "mlp", 5,
+        (low, low, wide, like((2, width), f32), like((owners, 3, units, width), bf16), like((2, full), f32)),
+        (IN_VMEM,) * 6, [IN_VMEM] * 9, scratch,
+        branch, tokens, alpha_attn, alpha_mlp, cotangent, up_gate, down, up_scale, gate_scale,
     )
 
 
@@ -499,11 +1066,16 @@
     tokens, lengths, w_query, w_key, w_value, s_qk, w_out, up_weight, gate_weight, down_weight,
     s_up, s_gate, alpha_attn, alpha_mlp, cotangent,
 ):
+    outer = lax.axis_size("o")
+    own_units = up_weight.shape[0]
+    if outer > 1:
+        up_weight, gate_weight, down_weight, s_up, s_gate = (
+            gather(a, "o") for a in (up_weight, gate_weight, down_weight, s_up, s_gate)
+        )
     units = up_weight.shape[0]
-    mlp_scale = gather(jnp.stack([s_up, s_gate])[None], OWNERS).astype(f32)
-    owners = mlp_scale.shape[0]
-    down_full = gather(down_weight, OWNERS)
-    up_scale, gate_scale = (mlp_scale[:, i].reshape(1, owners * units) for i in range(2))
+    scales = jnp.zeros((2, SCALE_ROWS, up_weight.shape[1]), bf16)
+    scales = scales.at[:, 0, :units].set(jnp.stack([s_up, s_gate]))
+    up_gate = jnp.concatenate([jnp.stack([up_weight, gate_weight]), scales], axis=1)
 
     length = lax.axis_size("z")
     own_rows, width = tokens.shape
@@ -513,67 +1085,39 @@
     group_tokens, turned_q, turned_k, qt, kt, vt = project(
         length, tokens, joint, s_qk[:, None], cosine, sine
     )
-    up_gate = jnp.stack([up_weight, gate_weight])[None]
-    qt, up_gate = lax.optimization_barrier((qt, up_gate))
-    up_gate = gather(up_gate, OWNERS)
-    up_full, gate_full = (up_gate[:, i].reshape(owners * units, -1) for i in range(2))
     ot, lse = attention_forward(lengths, qt, kt, vt)
-    branch = branch_sum(length, ot, w_out, own_rows)
-
-    hidden, front_pull = jax.vjp(front, branch, tokens.astype(f32), alpha_attn)
-    hidden_low = gather(hidden.astype(bf16), PLANE)
-    up_proj = dot(hidden_low, up_full, 1, 1)
-    gate_proj = dot(hidden_low, gate_full, 1, 1)
-    inner, core_pull = jax.vjp(core, up_proj, gate_proj, up_scale, gate_scale)
-    inner_low = inner.astype(bf16)
-    mlp_out = scatter_sum(dot(inner_low, down_full, 1, 0).astype(bf16), PLANE).astype(f32)
-    mixed, finish_pull = jax.vjp(front, mlp_out, hidden, alpha_mlp)
-    mlp_out_grad, hidden_grad, alpha_mlp_grad = finish_pull(cotangent.astype(f32))
-    mlp_out_low = gather(mlp_out_grad.astype(bf16), PLANE)
-    down_grad = dot(inner_low, mlp_out_low, 0, 0)
-    up_proj_grad, gate_proj_grad, up_scale_grad, gate_scale_grad = core_pull(
-        dot(mlp_out_low, down_full, 1, 1)
-    )
-    up_low, gate_low = up_proj_grad.astype(bf16), gate_proj_grad.astype(bf16)
-    hidden_part = dot(up_low, up_full, 1, 0) + dot(gate_low, gate_full, 1, 0)
-    hidden_grad = hidden_grad + scatter_sum(hidden_part.astype(bf16), PLANE).astype(f32)
-    up_grad = dot(up_low, hidden_low, 0, 0)
-    gate_grad = dot(gate_low, hidden_low, 0, 0)
-    mlp_grads = jnp.stack(
-        [g.astype(bf16).reshape(owners, units, -1) for g in (up_grad, gate_grad, down_grad)], 1
-    )
-    mlp_grads = scatter_sum(mlp_grads, OWNERS)[0].astype(f32)
-    scale_grads = jnp.stack(
-        [g.reshape(owners, units) for g in (up_scale_grad, gate_scale_grad)], axis=1
-    )
-    scale_grads = scatter_sum(scale_grads, OWNERS)[0]
-    branch_grad, token_grad, alpha_attn_grad = front_pull(hidden_grad)
-
-    got, out_grad = spread(length, branch_grad.astype(bf16), w_out, ot)
+    branch, up_gate = branch_sum(length, ot, w_out, up_gate, own_rows)
+    up_scale, gate_scale = (up_gate[:, i, units, :units].reshape(1, -1).astype(f32) for i in range(2))
+    mixed, branch_low, token_grad, alpha_grads, mlp_grads, scale_grads = mlp(
+        length, branch, tokens, alpha_attn[None], alpha_mlp[None], cotangent, up_gate, down_weight,
+        up_scale, gate_scale,
+    )
+    got, out_grad, mlp_grads = spread(length, branch_low, w_out, ot, mlp_grads)
     gqt, gkt, gvt = attention_backward(lengths, qt, kt, vt, ot, got, lse)
-    gqt, query_gain_grad = features_back(turned_q, s_qk, gqt * (1.0 / ROOT), cosine, sine)
-    gkt, key_gain_grad = features_back(turned_k, s_qk, gkt * (1.0 / ROOT), cosine, sine)
-    joint_grad = jnp.concatenate([gqt, gkt, gvt], axis=0).astype(bf16)
-    token_attn_grad = token_sum(length, joint_grad, joint, own_rows)
-    joint_weight_grad = dot(group_tokens.reshape(rows, width), joint_grad, 0, 1)
-    dp = ("o", "x")
-    joint_weight_grad = lax.psum(joint_weight_grad.astype(bf16), dp).astype(f32)
-    out_grad = lax.psum(out_grad.astype(bf16), dp).astype(f32)
-    gain_grad = lax.psum(query_gain_grad + key_gain_grad, dp)
-    alpha_sums = lax.psum(jnp.stack([alpha_attn_grad, alpha_mlp_grad]), AXES)
+    tokens_grad, attn_grads, alpha_sums, scale_sums, gain_grad = inward(
+        length, group_tokens, token_grad, out_grad, alpha_grads, scale_grads,
+        gqt, gkt, gvt, turned_q, turned_k, s_qk[:, None], cosine, sine, joint,
+    )
+    if outer > 1:
+        mlp_grads = lax.psum_scatter(mlp_grads, "o", scatter_dimension=1, tiled=True)
+        attn_grads, alpha_sums, scale_sums, gain_grad = lax.psum(
+            (attn_grads, alpha_sums, scale_sums, gain_grad), "o"
+        )
+    place = lax.axis_index("z") * units + lax.axis_index("o") * own_units
+    scale_sums = lax.dynamic_slice_in_dim(scale_sums, place, own_units, 1)
     return (
-        mixed.astype(bf16),
-        (token_grad + token_attn_grad).astype(bf16),
-        joint_weight_grad[:, :HEAD_DIM],
-        joint_weight_grad[:, HEAD_DIM : 2 * HEAD_DIM],
-        joint_weight_grad[:, 2 * HEAD_DIM :],
-        gain_grad,
-        out_grad,
+        mixed,
+        tokens_grad,
+        attn_grads[:HEAD_DIM].T,
+        attn_grads[HEAD_DIM : 2 * HEAD_DIM].T,
+        attn_grads[2 * HEAD_DIM : 3 * HEAD_DIM].T,
+        gain_grad[:, 0],
+        attn_grads[3 * HEAD_DIM :],
         mlp_grads[0],
         mlp_grads[1],
         mlp_grads[2],
-        scale_grads[0],
-        scale_grads[1],
+        scale_sums[0],
+        scale_sums[1],
         alpha_sums[0],
         alpha_sums[1],
     )

time: 698 us -> 433 us (0.62)
  waiting for transfers between devices: 217 us -> 0 us
  Pallas kernels: 278 us -> 409 us
  blocking collectives: 68.7 us -> 0 us
  matrix products: 51.6 us -> 0 us
  other arithmetic: 44.8 us -> 7.39 us
  between operations: 15.2 us -> 1.28 us
    reduce_scatter x3 -> x0, waiting for transfers between devices: 139 us -> none  [scatter_sum(): return lax.psum_scatter(values, axes, scatter_dimension=0, tiled=True)]
    pallas_call x4 -> x5, Pallas kernels: 252 us -> 383 us  [remote_call(): pl.pallas_call(kernel, name=name, out_shape=outs, in_specs=in_specs, out_...]
    all_gather x4 -> x0, waiting for transfers between devices: 77.1 us -> none  [gather(): return lax.all_gather(values, axes, axis=0, tiled=True)]
    dot_general x10 -> x0, matrix products: 51.6 us -> none  [dot(): lax.dot_general(left, right, (((left_dim,), (right_dim,)), ((), ())), pre...]
    psum x2 -> x0, blocking collectives: 45 us -> none  [the longest x1 39.6 us: shards(): alpha_sums = lax.psum(jnp.stack([alpha_attn_grad, alpha_mlp_grad]), AXES)]
    reduce_sum x9 -> x0, other arithmetic: 15.8 us -> none  [the longest x3 4.35 us: sphere(): jnp.mean(values * values, axis=-1, keepdims=True) + EPSILON]
    unnamed x1 -> x0, blocking collectives: 12.1 us -> none
    all_gather x1 -> x0, blocking collectives: 11.6 us -> none  [gather(): return lax.all_gather(values, axes, axis=0, tiled=True)]
  transfers between devices with their start and end apart: 8 -> 0, of which waited for: 6 -> 0; matrix products, arithmetic and copies ran while one was open for 5% -> 0% of each run, Pallas kernels for 20% -> 0%
where the time goes in v3:
time: 433 us; the launch traced here: 425 us
  Pallas kernels  409 us (94%)
  local copies, waits for them, and re-layouts  7.91 us (2%)
  other arithmetic  7.39 us (2%)
    pallas_call x5, Pallas kernels, remote_call(): pl.pallas_call(kernel, name=name, out_shape=outs, in_specs=in_specs, out_...  383 us
    pallas_call x2, Pallas kernels, attention_call(): pl.pallas_call(kernel, name=name, out_shape=outs, in_specs=[pl.BlockSpec(...  26 us

profile of v3, /device:TPU:0, one launch (start us, length us, event | category | flops | bytes accessed | tf_op | source)
XLA Modules:
  0.0 425.2 jit_solution(6246826712751675634)
XLA Ops:
  0.6 0.0 copy-start.7
  0.7 0.0 copy-start.6
  0.7 0.0 copy-start.5
  0.7 0.0 copy-start.10
  0.7 0.8 select_reduce_fusion.1
  1.5 0.1 select_reduce_fusion
  1.7 2.8 multiply_sine_fusion
  4.5 0.0 copy-done.7
  4.5 0.0 copy-done.6
  4.5 0.0 copy-done.5
  4.5 0.8 maximum_bitcast_fusion.joint
  5.3 0.0 copy-done.10
  5.3 0.7 copy.34.gain
  6.0 62.8 %project.1 = (bf16[8,512,1024]{2,1,0:T(8,128)(2,1)}, f32[64,4096]{1,0:T(8,128)}, f32[64,4096]{1,0:T(8,128)}, bf16[64,4096]{1,0:T(8,128)(2,1)}, bf16[64,4096]{1,0:T(8,128)(2,1)}, /*index=5*/bf16[64,4096]{1,0:T(8,128)(2,1)}) custom-call(bf16[256,1024]{1,0:T(8,128)(2,1)} %tokens.3, bf16[192,1024]{1,0:T(8,128)(2,1)} %maximum_bitcast_fusion.joint, ...), custom_call_target="tpu_custom_call" | custom-call | tf_op jit(solution)/shard_map/project/pallas_call | solution.py:362
  68.8 0.0 copy-start.11
  68.8 0.0 copy-start.12
  68.8 0.0 copy-start.3
  68.8 0.0 copy-start.4
  68.8 9.5 %attn_forward.1 = (bf16[64,4096]{1,0:T(8,128)(2,1)}, f32[1,4096]{1,0:T(1,128)}) custom-call(s32[1,4]{1,0:T(1,128)} %lengths.3, bf16[64,4096]{1,0:T(8,128)(2,1)} %get-tuple-element.53.qt, bf16[64,4096]{1,0:T(8,128)(2,1)} %get-tuple-element.54.kt, bf16[64,4096]{1,0:T(8,128)(2,1)} %get-tuple-element.55.vt), custom_call_target="tpu_custom_call" | custom-call | tf_op jit(solution)/shard_map/attn_forward/pallas_call | solution.py:107
  78.3 0.0 copy-done.11
  78.3 0.0 copy-done.12
  78.4 0.0 copy-done.3
  78.4 0.0 copy-done.4
  78.4 0.9 fusion.1.weight
  79.3 70.3 %branch_sum.1 = (f32[256,1024]{1,0:T(8,128)}, bf16[4,2,144,1024]{3,2,1,0:T(8,128)(2,1)}) custom-call(bf16[64,4096]{1,0:T(8,128)(2,1)} %get-tuple-element.56.ot, bf16[64,1024]{1,0:T(8,128)(2,1)} %w_out.3, bf16[2,144,1024]{2,1,0:T(8,128)(2,1)} %fusion.1.weight), custom_call_target="tpu_custom_call" | custom-call | tf_op jit(solution)/shard_map/branch_sum/pallas_call | solution.py:362
  149.6 1.3 bitcast_convert_fusion
  150.9 106.0 %mlp.1 = (bf16[256,1024]{1,0:T(8,128)(2,1)}, bf16[256,1024]{1,0:T(8,128)(2,1)}, f32[256,1024]{1,0:T(8,128)}, f32[2,1024]{1,0:T(2,128)}, bf16[4,3,128,1024]{3,2,1,0:T(8,128)(2,1)}, /*index=5*/f32[2,512]{1,0:T(2,128)}) custom-call(f32[256,1024]{1,0:T(8,128)} %get-tuple-element.57.branch, bf16[256,1024]{1,0:T(8,128)(2,1)} %tokens.3, f32[1,1024]{1,0:T(1,128)} %bitcast.40, ...), custom_call_target="tpu_custom_call" | custom-call | tf_op jit(solution)/shard_map/mlp/pallas_call | solution.py:362
  256.9 80.6 %spread.1 = (bf16[64,4096]{1,0:T(8,128)(2,1)}, f32[64,1024]{1,0:T(8,128)}, f32[3,128,1024]{2,1,0:T(8,128)}) custom-call(bf16[256,1024]{1,0:T(8,128)(2,1)} %get-tuple-element.60.grad, bf16[64,1024]{1,0:T(8,128)(2,1)} %w_out.3, bf16[64,4096]{1,0:T(8,128)(2,1)} %get-tuple-element.56.ot, bf16[4,3,128,1024]{3,2,1,0:T(8,128)(2,1)} %get-tuple-element.61.parts), custom_call_target="tpu_custom_call" | custom-call | tf_op jit(solution)/shard_map/spread/pallas_call | solution.py:362
  337.5 16.5 %attn_backward.1 = (f32[64,4096]{1,0:T(8,128)}, f32[64,4096]{1,0:T(8,128)}, f32[64,4096]{1,0:T(8,128)}) custom-call(s32[1,4]{1,0:T(1,128)} %lengths.3, bf16[64,4096]{1,0:T(8,128)(2,1)} %get-tuple-element.53.qt, bf16[64,4096]{1,0:T(8,128)(2,1)} %get-tuple-element.54.kt, bf16[64,4096]{1,0:T(8,128)(2,1)} %get-tuple-element.55.vt, ...), custom_call_target="tpu_custom_call" | custom-call | tf_op jit(solution)/shard_map/attn_backward/pallas_call | solution.py:107
  354.0 62.9 %inward.1 = (bf16[256,1024]{1,0:T(8,128)(2,1)}, f32[256,1024]{1,0:T(8,128)}, f32[2,1024]{1,0:T(2,128)}, f32[2,512]{1,0:T(2,128)}, f32[64,1]{1,0:T(8,128)}) custom-call(f32[64,4096]{1,0:T(8,128)} %get-tuple-element.64.gqt, f32[64,4096]{1,0:T(8,128)} %get-tuple-element.65.gkt, f32[64,4096]{1,0:T(8,128)} %get-tuple-element.66.gvt, ...), custom_call_target="tpu_custom_call" | custom-call | tf_op jit(solution)/shard_map/inward/pallas_call | solution.py:362
  416.9 0.0 copy-start.9
  416.9 0.0 copy-start.8
  417.0 0.0 copy-start
  417.0 2.3 fusion.5
  419.3 0.6 constant_dynamic-slice_fusion
  419.9 0.5 slice_bitcast_fusion.6
  420.4 0.0 copy-done.9
  420.4 0.6 fusion.6
  421.0 0.0 copy-done.8
  421.0 0.6 reduce.2
  421.7 0.0 copy-done
  421.7 0.0 copy-start.1
  421.7 1.2 slice_bitcast_fusion
  422.8 0.0 copy-start.2
  422.8 0.1 copy-done.1
  423.0 0.8 copy.39
  423.8 0.2 copy-done.2
  424.0 0.8 copy.40
  (5 shorter events, 0.0 us)
Async XLA Ops:
  0.6 3.9 copy-start.7
  0.7 3.9 copy-start.6
  0.7 3.8 copy-start.5
  0.7 4.6 %copy-start.10 = (f32[64]{0:T(128)S(1)}, f32[64]{0:T(128)}, u32[]{:S(2)}) copy-start(f32[64]{0:T(128)} %param.22) | copy-start | bytes 772
  68.8 9.5 %copy-start.11 = (bf16[128]{0:T(256)(128)(2,1)S(1)}, bf16[128]{0:T(256)(128)(2,1)}, u32[]{:S(2)}) copy-start(bf16[128]{0:T(256)(128)(2,1)} %param.28) | copy-start | bytes 772
  68.8 9.5 %copy-start.12 = (bf16[128]{0:T(256)(128)(2,1)S(1)}, bf16[128]{0:T(256)(128)(2,1)}, u32[]{:S(2)}) copy-start(bf16[128]{0:T(256)(128)(2,1)} %param.27) | copy-start | bytes 772
  68.8 9.6 %copy-start.3 = (bf16[128,1024]{1,0:T(8,128)(2,1)S(1)}, bf16[128,1024]{1,0:T(8,128)(2,1)}, u32[]{:S(2)}) copy-start(bf16[128,1024]{1,0:T(8,128)(2,1)} %param.25) | copy-start | bytes 786436
  68.8 9.6 %copy-start.4 = (bf16[128,1024]{1,0:T(8,128)(2,1)S(1)}, bf16[128,1024]{1,0:T(8,128)(2,1)}, u32[]{:S(2)}) copy-start(bf16[128,1024]{1,0:T(8,128)(2,1)} %param.24) | copy-start | bytes 786436
  416.9 3.5 copy-start.9
  416.9 4.1 copy-start.8
  417.0 4.7 %copy-start = (f32[3,128,1024]{2,1,0:T(8,128)S(1)}, f32[3,128,1024]{2,1,0:T(8,128)}, u32[]{:S(2)}) copy-start(f32[3,128,1024]{2,1,0:T(8,128)} %get-tuple-element.77) | copy-start | bytes 4718596
  421.7 1.3 copy-start.1
  422.8 1.1 copy-start.2
